TPU v7x, 32 devices: a whole 2x2x4 slice. The times are simulated.
32 devices in a mesh: seq: 8 (over z, core), kvh: 4 (over y, x).
Axes of the slice: x: 2, y: 2, z: 4, core: 2. Of those that a mesh axis runs over, the one named last changes fastest.
Arguments:
- normed: bfloat16 [2048, 4096], P('seq'), may hold values from -8 to 8
- w_query: bfloat16 [4096, 4096], P(None, 'kvh'), may hold values from -1 to 1, as said below
- w_key: bfloat16 [4096, 1024], P(None, 'kvh'), may hold values from -1 to 1, as said below
- w_value: bfloat16 [4096, 1024], P(None, 'kvh'), may hold values from -0.09375 to 0.09375
- positions: int32 [2048], P('seq'), may hold values from 0 to 2174, as said below
- block_mask: int32 [16, 16], P('seq'), may hold values from 0 to 1, as said below
- grad_attn: bfloat16 [2048, 4096], P('seq', 'kvh'), may hold values from -6 to 6
Outputs:
- grad_normed: bfloat16 [2048, 4096], P('seq', 'kvh')
- grad_wq: float32 [4096, 4096], P('seq', 'kvh')
- grad_wk: float32 [4096, 1024], P('seq', 'kvh')
- grad_wv: float32 [4096, 1024], P('seq', 'kvh')
Inputs may be any that keep to these rules, and one draw needn't show every extreme that they name: Within a block positions rise by one per token; block b starts between b * 128 and (b + 1) * 128 - 1, block 0 at 0, the last block at its latest start. `block_mask`: the diagonal is 1; a block may read only blocks of earlier rounds besides itself; entries for earlier rounds are 0 or 1. `w_query`: entries of about 4096^(-1/2) in size. `w_key`: entries of about 4096^(-1/2) in size.
All inputs are finite; a program needn't handle non-finite values.
Results may differ from a plain program's by a relative error of at most 0.019.
The roundings to bfloat16 on the way count: a program that leaves them out, or rounds other values in their place, can miss the bound.
Values may be sent and summed in bfloat16 or wider, within the bound.
A program may use at most 128 MiB of HBM per device.

v0:
```python
import jax
import jax.numpy as jnp
from jax import lax
from jax.sharding import PartitionSpec as P

HEAD = 128
BLOCK = 128


THETA = 500000.0


def rotate(values, positions, rotation_sign):
    tok_rows = values.shape[0]
    head_count = values.shape[1] // HEAD
    half_size = HEAD // 2
    pieces = values.reshape(tok_rows, head_count, HEAD)
    frequency = THETA ** (-(jnp.arange(half_size, dtype=jnp.float32) * (2.0 / HEAD)))
    angles = positions.astype(jnp.float32)[:, None] * frequency[None, :]
    cosine = jnp.cos(angles)[:, None, :]
    sine_part = rotation_sign * jnp.sin(angles)[:, None, :]
    lower_half = pieces[:, :, :half_size]
    upper_half = pieces[:, :, half_size:]
    turned = jnp.concatenate(
        [
            lower_half * cosine - upper_half * sine_part,
            upper_half * cosine + lower_half * sine_part,
        ],
        axis=2,
    )
    return turned.reshape(tok_rows, head_count * HEAD)


def visible(mask_table, query_block0, query_count, key_count):
    query_local = jnp.arange(query_count)
    key_local = jnp.arange(key_count)
    query_block = query_block0 + query_local // BLOCK
    key_block = key_local // BLOCK
    allowed = jnp.repeat(jnp.repeat(mask_table, BLOCK, axis=0), BLOCK, axis=1) == 1
    inner_ok = (key_local % BLOCK)[None, :] <= (query_local % BLOCK)[:, None]
    return allowed & ((query_block[:, None] != key_block[None, :]) | inner_ok)


def product(form, left, right):
    return jnp.einsum(form, left, right, preferred_element_type=jnp.float32)


def masked_scores(queries, keys, seen):
    scores = product("tgd,sd->gts", queries, keys) * HEAD ** (-0.5)
    return jnp.where(seen[None], scores, -1e30)


def softmax_stats(queries, keys, values, grad_heads, seen):
    scores = masked_scores(queries, keys, seen)
    row_max = jnp.max(scores, axis=2, keepdims=True)
    log_total = row_max[:, :, 0] + jnp.log(jnp.sum(jnp.exp(scores - row_max), axis=2))
    weights = jnp.where(seen[None], jnp.exp(scores - log_total[:, :, None]), 0.0).astype(
        jnp.bfloat16
    )
    outputs = product("gts,sd->gtd", weights, values)
    row_dots = jnp.sum(outputs * jnp.transpose(grad_heads.astype(jnp.float32), (1, 0, 2)), axis=2)
    return (log_total, row_dots)


def attention_grads(queries, keys, values, grad_heads, seen, log_total, row_dots):
    scores = masked_scores(queries, keys, seen)
    probs = jnp.where(seen[None], jnp.exp(scores - log_total[:, :, None]), 0.0)
    weights = probs.astype(jnp.bfloat16)
    grad_probs = product("tgd,sd->gts", grad_heads, values)
    grad_scores = (probs * (grad_probs - row_dots[:, :, None]) * HEAD ** (-0.5)).astype(
        jnp.bfloat16
    )
    grad_query = product("gts,sd->tgd", grad_scores, keys)
    grad_key = product("gts,tgd->sd", grad_scores, queries)
    grad_value = product("gts,tgd->sd", weights, grad_heads)
    return (grad_query, grad_key, grad_value)


def body(normed, w_query, w_key, w_value, positions, block_mask, grad_attn):
    tok_rows = normed.shape[0]
    kv_local = w_key.shape[1] // HEAD
    group_size = w_query.shape[1] // w_key.shape[1]
    width_query = group_size * HEAD
    blk_local = tok_rows // BLOCK
    my_index = lax.axis_index("seq")
    queries = rotate(
        jnp.dot(normed, w_query, preferred_element_type=jnp.float32), positions, 1.0
    ).astype(jnp.bfloat16)
    keys = rotate(
        jnp.dot(normed, w_key, preferred_element_type=jnp.float32), positions, 1.0
    ).astype(jnp.bfloat16)
    values = jnp.dot(normed, w_value, preferred_element_type=jnp.float32).astype(jnp.bfloat16)
    keys_all, values_all = (
        lax.all_gather(keys, "seq", axis=0, tiled=True),
        lax.all_gather(values, "seq", axis=0, tiled=True),
    )
    seen = visible(block_mask, my_index * blk_local, tok_rows, keys_all.shape[0])
    query_parts = []
    key_parts = []
    value_parts = []
    total_parts = []
    dots_parts = []
    for head_index in range(kv_local):
        query_heads = queries[:, head_index * width_query : (head_index + 1) * width_query].reshape(
            tok_rows, group_size, HEAD
        )
        grad_heads = grad_attn[
            :, head_index * width_query : (head_index + 1) * width_query
        ].reshape(tok_rows, group_size, HEAD)
        key_head = keys_all[:, head_index * HEAD : (head_index + 1) * HEAD]
        value_head = values_all[:, head_index * HEAD : (head_index + 1) * HEAD]
        log_total, row_dots = softmax_stats(query_heads, key_head, value_head, grad_heads, seen)
        grad_query, grad_key, grad_value = attention_grads(
            query_heads, key_head, value_head, grad_heads, seen, log_total, row_dots
        )
        query_parts.append(grad_query.reshape(tok_rows, width_query))
        key_parts.append(grad_key)
        value_parts.append(grad_value)
        total_parts.append(log_total.T)
        dots_parts.append(row_dots.T)
    grad_queries = jnp.concatenate(query_parts, axis=1)
    key_total, value_total = (
        lax.psum_scatter(
            jnp.concatenate(key_parts, axis=1).astype(jnp.bfloat16),
            "seq",
            scatter_dimension=0,
            tiled=True,
        ).astype(jnp.float32),
        lax.psum_scatter(
            jnp.concatenate(value_parts, axis=1).astype(jnp.bfloat16),
            "seq",
            scatter_dimension=0,
            tiled=True,
        ).astype(jnp.float32),
    )
    query_grad = rotate(grad_queries, positions, -1.0).astype(jnp.bfloat16)
    key_grad = rotate(key_total, positions, -1.0).astype(jnp.bfloat16)
    value_grad = value_total.astype(jnp.bfloat16)
    joined = jnp.concatenate([query_grad, key_grad, value_grad], axis=1)
    weight_grads = lax.psum_scatter(
        lax.dot_general(
            normed, joined, (((0,), (0,)), ((), ())), preferred_element_type=jnp.float32
        ).astype(jnp.bfloat16),
        "seq",
        scatter_dimension=0,
        tiled=True,
    ).astype(jnp.float32)
    query_cols = query_grad.shape[1]
    key_cols = key_grad.shape[1]
    grad_wq = weight_grads[:, :query_cols]
    grad_wk = weight_grads[:, query_cols : query_cols + key_cols]
    grad_wv = weight_grads[:, query_cols + key_cols :]
    contract = (((1,), (1,)), ((), ()))
    partial_input = lax.dot_general(
        query_grad, w_query, contract, preferred_element_type=jnp.float32
    )
    partial_input = partial_input + lax.dot_general(
        key_grad, w_key, contract, preferred_element_type=jnp.float32
    )
    partial_input = partial_input + lax.dot_general(
        value_grad, w_value, contract, preferred_element_type=jnp.float32
    )
    grad_normed = lax.psum_scatter(
        partial_input.astype(jnp.bfloat16), "kvh", scatter_dimension=1, tiled=True
    )
    return (grad_normed, grad_wq, grad_wk, grad_wv)


def solution(mesh):
    in_specs = (
        P("seq", None),
        P(None, "kvh"),
        P(None, "kvh"),
        P(None, "kvh"),
        P("seq"),
        P("seq", None),
        P("seq", "kvh"),
    )
    out_specs = (P("seq", "kvh"), P("seq", "kvh"), P("seq", "kvh"), P("seq", "kvh"))
    return jax.shard_map(body, mesh=mesh, in_specs=in_specs, out_specs=out_specs, check_vma=False)
```

profile of v0, /device:TPU:0, one launch (start us, length us, event | category | flops | bytes accessed | tf_op | source)
XLA Modules:
  0.0 326.0 jit_solution(616527635279953923)
XLA Ops:
  7.2 0.0 all-gather.3.cloned.1.call-start
  7.2 0.8 convert_element_type.58
  8.1 0.3 multiply_sine_fusion
  8.4 0.4 copy-done
  8.8 2.5 fusion.44
  11.4 0.8 copy.77
  12.1 0.0 all-gather.3.cloned.1.call-update
  12.2 0.0 all-gather.5.cloned.1.call-start
  12.2 3.0 convolution_convert_fusion.1
  15.2 0.0 all-gather.5.cloned.1.call-update
  15.2 0.0 reduce-scatter.5.cloned.1.call-start
  15.3 6.8 %fusion.45 = f32[256,1024]{0,1:T(8,128)S(1)} fusion(bf16[256,4096]{1,0:T(8,128)(2,1)S(1)} %copy-done, bf16[4096,1024]{1,0:T(8,128)(2,1)} %param.8), kind=kOutput, calls=%fused_computation.100 | convolution fusion | flops 2147483648 | bytes 11534336 | tf_op jit(solution)/shard_map/reshape | solution.py:17
  22.1 0.2 subtract_convert_fusion.1
  22.3 0.7 fusion.43
  23.0 0.6 and_select_fusion
  23.6 0.1 copy.37
  23.7 0.1 broadcast_in_dim.84
  23.8 0.6 copy.87
  24.5 0.1 copy.84
  24.6 0.1 copy.83
  24.7 1.6 bitcast_and_fusion
  26.4 10.7 %all-gather.3.cloned.1.call-done = bf16[2048,256]{1,0:T(8,128)(2,1)} async-done(((bf16[256,256]{1,0:T(8,128)(2,1)}), bf16[2048,256]{1,0:T(8,128)(2,1)}) %all-gather.3.cloned.1.call-update) | async-done | bytes 1048592 | tf_op jit(solution)/shard_map/all_gather | solution.py:94
  37.1 2.6 fusion.9
  39.8 3.7 %exponential_reduce_fusion.1 = (f32[4,256]{1,0:T(4,128)S(1)}, f32[4,256]{1,0:T(4,128)S(1)}, f32[2048,256,4]{1,0,2:T(8,128)S(1)}) fusion(f32[2048,256,4]{1,0,2:T(8,128)S(1)} %get-tuple-element.32, f32[4,256]{1,0:T(4,128)S(1)} %get-tuple-element.31, pred[256,2048]{0,1:T(8,128)(4,1)S(1)} %bitcast_and_fusion, bf16[256,4,128]{0,2,1:T(8,128)(2,1)S(1)} %bitcast.151, ...), kind=kOutput, calls=%fused_computation.15 | convolution fusion | flops 551548928 | bytes 18100224 | tf_op jit(solution)/shard_map/tgd,sd->gts/dot_general | solution.py:45
  43.5 3.2 copy-done.1
  46.7 1.8 exponential_reduce_fusion
  48.6 12.5 %all-gather.5.cloned.1.call-done = bf16[2048,256]{1,0:T(8,128)(2,1)} async-done(((bf16[256,256]{1,0:T(8,128)(2,1)}), bf16[2048,256]{1,0:T(8,128)(2,1)}) %all-gather.5.cloned.1.call-update) | async-done | bytes 1048592 | tf_op jit(solution)/shard_map/all_gather | solution.py:95
  61.0 5.6 %fusion.16 = f32[4,256]{1,0:T(4,128)S(1)} fusion(bf16[256,4,128]{0,2,1:T(8,128)(2,1)S(1)} %bitcast.145, bf16[2048,256]{1,0:T(8,128)(2,1)} %all-gather.5.cloned.1.call-done, f32[2048,256,4]{1,0,2:T(8,128)} %copy-done.12, f32[4,256]{1,0:T(4,128)S(1)} %log_add_fusion.1, pred[256,2048]{0,1:T(8,128)(4,1)S(1)} %bitcast_and_fusion), kind=kOutput, calls=%fused_computation.36 | convolution fusion | flops 547748864 | bytes 9707520 | tf_op jit(solution)/shard_map/gts,sd->gtd/dot_general | solution.py:45
  66.6 0.7 copy-done.13
  67.3 3.5 %fusion.6 = bf16[4,256,2048]{1,2,0:T(8,128)(2,1)S(1)} fusion(f32[2048,256,4]{1,0,2:T(8,128)S(1)} %copy-done.13, bf16[256,4,128]{0,2,1:T(8,128)(2,1)S(1)} %bitcast.146, f32[4,256]{1,0:T(4,128)S(1)} %fusion.16, f32[4,256]{1,0:T(4,128)S(1)} %log_add_fusion.1, pred[256,2048]{0,1:T(8,128)(4,1)S(1)} %bitcast_and_fusion, bf16[2048,256]{1,0:T(8,128)(2,1)S(1)} %copy-done.10), kind=kOutput, calls=%fused_computation.10 | convolution fusion | flops 553648128 | bytes 13901824 | tf_op jit(solution)/shard_map/tgd,sd->gts/dot_general | solution.py:45
  70.8 1.5 fusion.12
  72.4 2.0 fusion.17
  74.4 3.3 %fusion.3 = bf16[4,256,2048]{1,2,0:T(8,128)(2,1)S(1)} fusion(f32[2048,256,4]{1,0,2:T(8,128)S(1)} %bitcast.136, bf16[256,4,128]{0,2,1:T(8,128)(2,1)S(1)} %bitcast.149, f32[4,256]{1,0:T(4,128)S(1)} %fusion.17, f32[4,256]{1,0:T(4,128)S(1)} %log_add_fusion, pred[256,2048]{0,1:T(8,128)(4,1)S(1)} %bitcast_and_fusion, bf16[2048,256]{1,0:T(8,128)(2,1)S(1)} %copy-done.10), kind=kOutput, calls=%fused_computation.5 | convolution fusion | flops 553648128 | bytes 13901824 | tf_op jit(solution)/shard_map/tgd,sd->gts/dot_general | solution.py:45
  77.7 1.9 copy-done.4
  79.7 1.5 fusion.13
  81.2 1.0 pad_maximum_fusion
  82.2 0.0 reduce-scatter.5.cloned.1.call-update
  82.2 0.0 reduce-scatter.7.cloned.1.call-start
  82.3 6.1 %fusion.15 = bf16[2048,128]{0,1:T(8,128)(2,1)S(1)} fusion(bf16[256,4,128]{0,2,1:T(8,128)(2,1)S(1)} %bitcast.150, f32[2048,256,4]{1,0,2:T(8,128)} %copy-done.1, f32[4,256]{1,0:T(4,128)S(1)} %log_add_fusion, pred[256,2048]{0,1:T(8,128)(4,1)S(1)} %bitcast_and_fusion), kind=kOutput, calls=%fused_computation.30 | convolution fusion | flops 547618816 | bytes 9703424 | tf_op jit(solution)/shard_map/gts,tgd->sd/dot_general | solution.py:45
  88.4 6.1 %fusion.14 = bf16[2048,128]{0,1:T(8,128)(2,1)S(1)} fusion(bf16[256,4,128]{0,2,1:T(8,128)(2,1)S(1)} %bitcast.147, f32[2048,256,4]{1,0,2:T(8,128)} %copy-done.12, f32[4,256]{1,0:T(4,128)S(1)} %log_add_fusion.1, pred[256,2048]{0,1:T(8,128)(4,1)S(1)} %bitcast_and_fusion), kind=kOutput, calls=%fused_computation.29 | convolution fusion | flops 547618816 | bytes 9703424 | tf_op jit(solution)/shard_map/gts,tgd->sd/dot_general | solution.py:45
  94.6 1.1 pad_maximum_fusion.1
  95.6 0.0 reduce-scatter.7.cloned.1.call-update
  95.7 0.0 reduce-scatter.11.cloned.1.call-start
  95.7 3.1 convolution_bitcast_fusion.5
  98.8 3.1 convolution_bitcast_fusion.4
  102.0 0.2 subtract_convert_fusion
  102.2 12.1 %reduce-scatter.5.cloned.1.call-done = bf16[256,256]{0,1:T(8,128)(2,1)} async-done(((bf16[2048,256]{0,1:T(8,128)(2,1)}), bf16[256,256]{0,1:T(8,128)(2,1)}) %reduce-scatter.5.cloned.1.call-update) | async-done | bytes 131088 | tf_op jit(solution)/shard_map/reduce_scatter | solution.py:123
  114.3 0.9 convert.51
  115.2 31.8 %reduce-scatter.7.cloned.1.call-done = bf16[256,256]{0,1:T(8,128)(2,1)} async-done(((bf16[2048,256]{0,1:T(8,128)(2,1)}), bf16[256,256]{0,1:T(8,128)(2,1)}) %reduce-scatter.7.cloned.1.call-update) | async-done | bytes 131088 | tf_op jit(solution)/shard_map/reduce_scatter | solution.py:129
  147.1 7.3 %fusion = bf16[4096,1536]{0,1:T(8,128)(2,1)} fusion(bf16[256,4096]{1,0:T(8,128)(2,1)S(1)} %copy-done, bf16[256,256]{0,1:T(8,128)(2,1)} %reduce-scatter.7.cloned.1.call-done, bf16[256,256]{0,1:T(8,128)(2,1)S(1)} %bitcast.140, bf16[256,1024]{0,1:T(8,128)(2,1)S(1)} %bitcast.137), kind=kOutput, calls=%fused_computation.1 | convolution fusion | flops 3229876224 | bytes 15466496 | tf_op jit(solution)/shard_map/dot_general | solution.py:141
  154.3 0.0 reduce-scatter.11.cloned.1.call-update
  154.3 0.0 reduce-scatter.9.cloned.1.call-start
  154.4 5.9 %fusion.46 = f32[256,4096]{1,0:T(8,128)S(1)} fusion(bf16[256,1024]{0,1:T(8,128)(2,1)S(1)} %bitcast.138, bf16[4096,1024]{1,0:T(8,128)(2,1)} %param.8), kind=kOutput, calls=%fused_computation.101 | convolution fusion | flops 2147483648 | bytes 13107200 | tf_op jit(solution)/shard_map/dot_general | solution.py:154
  160.4 0.8 convolution_add_fusion.1
  161.1 0.8 copy-done.5
  162.0 2.1 fusion.11
  164.1 0.0 reduce-scatter.9.cloned.1.call-update
  164.1 118.0 %reduce-scatter.11.cloned.1.call-done = bf16[512,1536]{0,1:T(8,128)(2,1)} async-done(((bf16[4096,1536]{0,1:T(8,128)(2,1)}), bf16[512,1536]{0,1:T(8,128)(2,1)}) %reduce-scatter.11.cloned.1.call-update) | async-done | bytes 1572880 | tf_op jit(solution)/shard_map/reduce_scatter | solution.py:140
  282.1 2.9 slice.90
  285.0 2.9 copy.58
  287.8 1.1 fusion.41
  289.0 1.0 copy.59
  290.0 1.0 copy.60
  291.0 28.1 %reduce-scatter.9.cloned.1.call-done = bf16[256,1024]{1,0:T(8,128)(2,1)} async-done(((bf16[256,4096]{1,0:T(8,128)(2,1)}), bf16[256,1024]{1,0:T(8,128)(2,1)}) %reduce-scatter.9.cloned.1.call-update) | async-done | bytes 524304 | tf_op jit(solution)/shard_map/reduce_scatter | solution.py:163
  (40 shorter events, 0.3 us)
Async XLA Ops:
  7.2 1.6 copy-start
  7.2 29.9 %all-gather.3.cloned.1.call-start = ((), (), s32[]{:S(2)}) async-start(), calls=%async_computation.4 | async-start | bytes 1179648 | tf_op jit(solution)/shard_map/all_gather | solution.py:94
  12.2 48.9 %all-gather.5.cloned.1.call-start = ((), (), s32[]{:S(2)}) async-start(), calls=%async_computation.5 | async-start | bytes 1179648 | tf_op jit(solution)/shard_map/all_gather | solution.py:95
  15.2 99.1 %reduce-scatter.5.cloned.1.call-start = ((), (), s32[]{:S(2)}) async-start(), calls=%async_computation.6 | async-start | bytes 1179648 | tf_op jit(solution)/shard_map/reduce_scatter | solution.py:123
  15.2 8.4 %copy-start.11 = (s32[2,16]{1,0:T(2,128)S(1)}, s32[2,16]{1,0:T(2,128)}, u32[]{:S(2)}) copy-start(s32[2,16]{1,0:T(2,128)} %param.12) | copy-start | bytes 388
  15.3 9.2 %copy-start.8 = (bf16[256,1024]{1,0:T(8,128)(2,1)S(1)}, bf16[256,1024]{1,0:T(8,128)(2,1)}, u32[]{:S(2)}) copy-start(bf16[256,1024]{1,0:T(8,128)(2,1)} %param.13) | copy-start | bytes 1572868
  37.1 2.6 copy-start.6
  39.7 3.7 %copy-start.12 = (f32[2048,256,4]{1,0,2:T(8,128)}, f32[2048,256,4]{1,0,2:T(8,128)S(1)}, u32[]{:S(2)}) copy-start(f32[2048,256,4]{1,0,2:T(8,128)S(1)} %get-tuple-element.32) | copy-start | bytes 25165828
  43.5 3.2 copy-start.1
  61.0 5.6 %copy-start.10 = (bf16[2048,256]{1,0:T(8,128)(2,1)S(1)}, bf16[2048,256]{1,0:T(8,128)(2,1)}, u32[]{:S(2)}) copy-start(bf16[2048,256]{1,0:T(8,128)(2,1)} %all-gather.5.cloned.1.call-done) | copy-start | bytes 3145732
  61.0 6.3 %copy-start.13 = (f32[2048,256,4]{1,0,2:T(8,128)S(1)}, f32[2048,256,4]{1,0,2:T(8,128)}, u32[]{:S(2)}) copy-start(f32[2048,256,4]{1,0,2:T(8,128)} %copy-done.12) | copy-start | bytes 25165828
  61.0 11.3 %slice-start = ((s8[8388608]{0:T(1024)(128)(4,1)}), s8[4194304]{0:T(1024)(128)(4,1)S(1)}, s32[]{:S(2)}) async-start(s8[8388608]{0:T(1024)(128)(4,1)} %bitcast.135), calls=%async_computation.10 | async-start | bytes 8388608
  67.3 3.5 %copy-start.9 = (bf16[256,512]{0,1:T(8,128)(2,1)S(1)}, bf16[256,512]{0,1:T(8,128)(2,1)}, u32[]{:S(2)}) copy-start(bf16[256,512]{0,1:T(8,128)(2,1)} %get-tuple-element.22) | copy-start | bytes 786436
  67.3 5.1 %slice-start.1 = ((s8[8388608]{0:T(1024)(128)(4,1)}), s8[4194304]{0:T(1024)(128)(4,1)S(1)}, s32[]{:S(2)}) async-start(s8[8388608]{0:T(1024)(128)(4,1)} %bitcast.135), calls=%async_computation.11 | async-start | bytes 8388608
  70.8 3.6 %copy-start.3 = (bf16[4,256,2048]{1,2,0:T(8,128)(2,1)}, bf16[4,256,2048]{1,2,0:T(8,128)(2,1)S(1)}, u32[]{:S(2)}) copy-start(bf16[4,256,2048]{1,2,0:T(8,128)(2,1)S(1)} %fusion.6) | copy-start | bytes 12582916
  77.7 2.0 copy-start.4
  82.2 64.8 %reduce-scatter.7.cloned.1.call-start = ((), (), s32[]{:S(2)}) async-start(), calls=%async_computation.7 | async-start | bytes 1179648 | tf_op jit(solution)/shard_map/reduce_scatter | solution.py:129
  95.7 186.4 %reduce-scatter.11.cloned.1.call-start = ((), (), s32[]{:S(2)}) async-start(), calls=%async_computation.9 | async-start | bytes 14155776 | tf_op jit(solution)/shard_map/reduce_scatter | solution.py:140
  154.3 164.8 %reduce-scatter.9.cloned.1.call-start = ((), (), s32[]{:S(2)}) async-start(), calls=%async_computation.8 | async-start | bytes 2621440 | tf_op jit(solution)/shard_map/reduce_scatter | solution.py:163
  154.4 5.9 %copy-start.2 = (bf16[4096,256]{1,0:T(8,128)(2,1)S(1)}, bf16[4096,256]{1,0:T(8,128)(2,1)}, u32[]{:S(2)}) copy-start(bf16[4096,256]{1,0:T(8,128)(2,1)} %param.9) | copy-start | bytes 6291460
  160.3 1.6 copy-start.5
  160.4 1.6 copy-start.7
Sparse Core Ops, SparseCore 0:
  12.3 24.7 all-gather.2
  39.3 21.7 all-gather.4
  82.4 31.8 reduce-scatter.4
  116.4 30.6 reduce-scatter.6
  154.5 127.5 reduce-scatter.10
  285.5 33.5 reduce-scatter.8
where the time goes:
time: 326 us
  waiting for transfers between devices  213 us (65%)
  matrix products  70.6 us (22%)
  local copies, waits for them, and re-layouts  18.6 us (6%)
  between operations  14.5 us (4%)
  other arithmetic  8.69 us (3%)
    reduce_scatter x1, waiting for transfers between devices, body(): lax.psum_scatter(lax.dot_general(normed, joined, (((0,), (0,)), ((), ()))...  118 us
    dot_general x12, matrix products, product(): return jnp.einsum(form, left, right, preferred_element_type=jnp.float32)  42.2 us
    reduce_scatter x1, waiting for transfers between devices, body(): lax.psum_scatter(jnp.concatenate(value_parts, axis=1).astype(jnp.bfloat16...  31.8 us
    reduce_scatter x1, waiting for transfers between devices, body(): lax.psum_scatter(partial_input.astype(jnp.bfloat16), 'kvh', scatter_dimen...  28.1 us
    unnamed x38, local copies, waits for them, and re-layouts  12.9 us
    all_gather x1, waiting for transfers between devices, body(): lax.all_gather(values, 'seq', axis=0, tiled=True)  12.5 us
    reduce_scatter x1, waiting for transfers between devices, body(): lax.psum_scatter(jnp.concatenate(key_parts, axis=1).astype(jnp.bfloat16),...  12.1 us
    all_gather x1, waiting for transfers between devices, body(): lax.all_gather(keys, 'seq', axis=0, tiled=True)  10.7 us
  transfers between devices with their start and end apart: 6, of which 6 were waited for; matrix products, arithmetic and copies ran while one was open for 19% of the time, Pallas kernels for 0%

commit v1 on v0

v1 whole, which is shorter than its diff:
```python
import functools
import math

import jax
import jax.numpy as jnp
from jax import lax
from jax.experimental import pallas as pl
from jax.experimental.pallas import tpu as pltpu
from jax.sharding import PartitionSpec as P

HEAD = 128
HALF = 64
BLOCK = 128
THETA = 500000.0
SCALE = HEAD**-0.5
LOG2E = math.log2(math.e)
MESH = pl.DeviceIdType.MESH
ANY = pl.BlockSpec(memory_space=pl.ANY)
VMEM = pl.BlockSpec(memory_space=pltpu.VMEM)


def params(collective=None, semantics=None):
    extra = {}
    if collective is not None:
        extra = dict(collective_id=collective, has_side_effects=True)
    if semantics is not None:
        extra["dimension_semantics"] = semantics
    return pltpu.CompilerParams(vmem_limit_bytes=56 * 1024 * 1024, **extra)


def gather_kernel(chips, own, out, local_sem, send_r, send_l, send_p, recv_l, recv_r, recv_p):
    me = lax.axis_index("seq")
    chip, core = me // 2, me % 2
    has_left, has_right = chip > 0, chip < chips - 1
    mine = pltpu.make_async_copy(own, out.at[me], local_sem)
    mine.start()
    barrier = pltpu.get_barrier_semaphore()

    def greet(device):
        pl.semaphore_signal(barrier, inc=1, device_id={"seq": device}, device_id_type=MESH)

    greet(chip * 2 + 1 - core)
    pl.when(has_left)(lambda: greet(me - 2))
    pl.when(has_right)(lambda: greet(me + 2))
    pl.semaphore_wait(barrier, 1 + has_left.astype(jnp.int32) + has_right.astype(jnp.int32))

    def remote(src, slot, send, recv, device):
        return pltpu.make_async_remote_copy(
            src_ref=src,
            dst_ref=out.at[slot],
            send_sem=send,
            recv_sem=recv,
            device_id={"seq": device},
            device_id_type=MESH,
        )

    def source(distance, slot):
        return own if distance == 0 else out.at[slot]

    def right(t):
        slot = me - 2 * t
        return remote(source(t, slot), slot, send_r.at[t], recv_l.at[t + 1], me + 2)

    def left(t):
        slot = me + 2 * t
        return remote(source(t, slot), slot, send_l.at[t], recv_r.at[t + 1], me - 2)

    def partner(offset):
        slot = me + 2 * offset
        at = offset + chips - 1
        return remote(
            source(abs(offset), slot), slot, send_p.at[at], recv_p.at[at], chip * 2 + 1 - core
        )

    def arrival(slot, sem):
        pltpu.make_async_copy(out.at[slot], out.at[slot], sem).wait()

    pl.when(has_right)(lambda: right(0).start())
    pl.when(has_left)(lambda: left(0).start())
    partner(0).start()
    for t in range(1, chips):

        @pl.when(chip - t >= 0)
        def _():
            arrival(me - 2 * t, recv_l.at[t])
            if t < chips - 1:
                pl.when(has_right)(lambda: right(t).start())
            partner(-t).start()

        @pl.when(chip + t < chips)
        def _():
            arrival(me + 2 * t, recv_r.at[t])
            if t < chips - 1:
                pl.when(has_left)(lambda: left(t).start())
            partner(t).start()

    mine.wait()
    other = chip * 2 + 1 - core
    for t in range(chips):

        @pl.when(chip - t >= 0)
        def _():
            arrival(other - 2 * t, recv_p.at[chips - 1 - t])
            partner(-t).wait_send()
            if t < chips - 1:
                pl.when(has_right)(lambda: right(t).wait_send())

        @pl.when(chip + t < chips)
        def _():
            if t > 0:
                arrival(other + 2 * t, recv_p.at[chips - 1 + t])
                partner(t).wait_send()
            if t < chips - 1:
                pl.when(has_left)(lambda: left(t).wait_send())


def gather(block, devices, collective):
    chips = devices // 2
    dma = pltpu.SemaphoreType.DMA
    out = pl.pallas_call(
        functools.partial(gather_kernel, chips),
        out_shape=jax.ShapeDtypeStruct((devices,) + block.shape, block.dtype),
        in_specs=[ANY],
        out_specs=ANY,
        scratch_shapes=[
            dma(()),
            dma((chips,)),
            dma((chips,)),
            dma((2 * chips,)),
            dma((chips + 1,)),
            dma((chips + 1,)),
            dma((2 * chips,)),
        ],
        compiler_params=params(collective),
        cost_estimate=pl.CostEstimate(
            flops=0, bytes_accessed=24 * devices * block.size, transcendentals=0
        ),
    )(block)
    return out.reshape(devices * block.shape[0], block.shape[1])


def reduce_kernel(
    chips, part, out, from_partner, summed, arrived, send_p, recv_p, send_z, recv_z
):
    me = lax.axis_index("seq")
    chip, core = me // 2, me % 2
    other = chip * 2 + 1 - core
    barrier = pltpu.get_barrier_semaphore()

    def greet(device):
        pl.semaphore_signal(barrier, inc=1, device_id={"seq": device}, device_id_type=MESH)

    greet(other)
    for t in range(1, chips):
        greet(((chip + t) % chips) * 2 + core)
    pl.semaphore_wait(barrier, chips)

    def to_partner(t):
        return pltpu.make_async_remote_copy(
            src_ref=part.at[((chip + t) % chips) * 2 + 1 - core],
            dst_ref=from_partner.at[t],
            send_sem=send_p.at[t],
            recv_sem=recv_p.at[t],
            device_id={"seq": other},
            device_id_type=MESH,
        )

    def to_owner(t):
        return pltpu.make_async_remote_copy(
            src_ref=summed.at[t],
            dst_ref=arrived.at[t],
            send_sem=send_z.at[t],
            recv_sem=recv_z.at[t],
            device_id={"seq": ((chip + t) % chips) * 2 + core},
            device_id_type=MESH,
        )

    order = list(range(1, chips)) + [0]
    for t in order:
        to_partner(t).start()
    for t in order:
        to_partner(t).wait()
        total = part[((chip + t) % chips) * 2 + core].astype(jnp.float32) + from_partner[t].astype(
            jnp.float32
        )
        if t:
            summed[t] = total.astype(summed.dtype)
            to_owner(t).start()
        else:
            out[...] = total
    for t in range(1, chips):
        to_owner(t).wait()
        out[...] += arrived[t].astype(jnp.float32)


def reduce_to_owner(part, devices, collective):
    chips = devices // 2
    rows, cols = part.shape[0] // devices, part.shape[1]
    dma = pltpu.SemaphoreType.DMA((chips,))
    slots = pltpu.VMEM((chips, rows, cols), part.dtype)
    return pl.pallas_call(
        functools.partial(reduce_kernel, chips),
        out_shape=jax.ShapeDtypeStruct((rows, cols), jnp.float32),
        in_specs=[VMEM],
        out_specs=VMEM,
        scratch_shapes=[slots, slots, slots, dma, dma, dma, dma],
        compiler_params=params(collective),
        cost_estimate=pl.CostEstimate(
            flops=0, bytes_accessed=24 * part.size, transcendentals=0
        ),
    )(part.reshape(devices, rows, cols))


def dot(left, right, contract):
    return lax.dot_general(
        left, right, ((contract[:1], contract[1:]), ((), ())), preferred_element_type=jnp.float32
    )


def attention_kernel(
    group, chunk, mask, first, q, g, k, v, cos_t, sin_t, dq, dk, dv, bias, scores, gprobs, weights,
    k_t, dk_sum, dv_sum
):
    step = pl.program_id(0)
    keys, tokens = bias.shape
    chunks = [pl.ds(c * chunk, chunk) for c in range(keys // chunk)]

    @pl.when(step == 0)
    def _():
        key_at = lax.broadcasted_iota(jnp.int32, (BLOCK, BLOCK), 0)
        query_at = lax.broadcasted_iota(jnp.int32, (BLOCK, BLOCK), 1)
        lower = jnp.where(key_at <= query_at, 0.0, -1e30).astype(jnp.float32)
        for i in range(tokens // BLOCK):
            def fill(j, _, i=i):
                shown = jnp.where(mask[i, j] == 1, 0.0, -1e30).astype(jnp.float32)
                inner = jnp.where(j == first[0] + i, 1.0, 0.0).astype(jnp.float32)
                rows = pl.ds(pl.multiple_of(j * BLOCK, BLOCK), BLOCK)
                bias[rows, i * BLOCK : (i + 1) * BLOCK] = lower * inner + shown
                return 0

            lax.fori_loop(0, keys // BLOCK, fill, 0)

    @pl.when(step % group == 0)
    def _():
        k_t[...] = k[...].T
        dk_sum[...] = jnp.zeros_like(dk_sum)
        dv_sum[...] = jnp.zeros_like(dv_sum)

    qh, gh = q[...], g[...]
    top = jnp.full((1, tokens), -3e38, jnp.float32)
    for at in chunks:
        s = dot(k[at, :], qh, (1, 1)) * (SCALE * LOG2E) + bias[at, :]
        scores[at, :] = s
        gprobs[at, :] = dot(v[at, :], gh, (1, 1))
        top = jnp.maximum(top, jnp.max(s, axis=0, keepdims=True))
    total = jnp.zeros((1, tokens), jnp.float32)
    for at in chunks:
        e = jnp.exp2(scores[at, :] - top)
        scores[at, :] = e
        total = total + jnp.sum(e, axis=0, keepdims=True)
    inverse = 1.0 / total
    row_dots = jnp.zeros((1, tokens), jnp.float32)
    for at in chunks:
        w = (scores[at, :] * inverse).astype(jnp.bfloat16)
        weights[at, :] = w
        row_dots = row_dots + jnp.sum(
            w.astype(jnp.float32) * gprobs[at, :], axis=0, keepdims=True
        )
    inverse_scaled = inverse * SCALE
    dq_t = jnp.zeros((HEAD, tokens), jnp.float32)
    for at in chunks:
        ds = ((scores[at, :] * inverse_scaled) * (gprobs[at, :] - row_dots)).astype(jnp.bfloat16)
        dk_sum[at, :] += dot(ds, qh, (1, 0))
        dv_sum[at, :] += dot(weights[at, :], gh, (1, 0))
        dq_t = dq_t + dot(k_t[:, at], ds, (1, 0))
    low, high = dq_t[:HALF, :], dq_t[HALF:, :]
    c, s = cos_t[...], sin_t[...]
    turned = jnp.concatenate([low * c + high * s, high * c - low * s], axis=0)
    dq[...] = turned.T.astype(jnp.bfloat16)

    @pl.when(step % group == group - 1)
    def _():
        dk[...] = dk_sum[...].astype(jnp.bfloat16)
        dv[...] = dv_sum[...].astype(jnp.bfloat16)


def attention(queries, grad_attn, keys_values, mask, first, cos_t, sin_t, kv_local):
    tokens = queries.shape[0]
    heads = queries.shape[1] // HEAD
    group = heads // kv_local
    keys = keys_values.shape[0]
    f32, bf16 = jnp.float32, jnp.bfloat16
    one_head = pl.BlockSpec((tokens, HEAD), lambda h: (0, h))
    angle = pl.BlockSpec((HALF, tokens), lambda h: (0, 0))
    smem = pl.BlockSpec(memory_space=pltpu.SMEM)
    return pl.pallas_call(
        functools.partial(attention_kernel, group, 512),
        grid=(heads,),
        out_shape=[
            jax.ShapeDtypeStruct((tokens, heads * HEAD), bf16),
            jax.ShapeDtypeStruct((keys, kv_local * HEAD), bf16),
            jax.ShapeDtypeStruct((keys, kv_local * HEAD), bf16),
        ],
        in_specs=[
            smem,
            smem,
            one_head,
            one_head,
            pl.BlockSpec((keys, HEAD), lambda h: (0, h // group)),
            pl.BlockSpec((keys, HEAD), lambda h: (0, kv_local + h // group)),
            angle,
            angle,
        ],
        out_specs=[
            one_head,
            pl.BlockSpec((keys, HEAD), lambda h: (0, h // group)),
            pl.BlockSpec((keys, HEAD), lambda h: (0, h // group)),
        ],
        scratch_shapes=[
            pltpu.VMEM((keys, tokens), f32),
            pltpu.VMEM((keys, tokens), f32),
            pltpu.VMEM((keys, tokens), f32),
            pltpu.VMEM((keys, tokens), bf16),
            pltpu.VMEM((HEAD, keys), bf16),
            pltpu.VMEM((keys, HEAD), f32),
            pltpu.VMEM((keys, HEAD), f32),
        ],
        compiler_params=params(None, ("arbitrary",)),
        cost_estimate=pl.CostEstimate(
            flops=10 * keys * tokens * heads * HEAD,
            bytes_accessed=8 * keys * HEAD * kv_local,
            transcendentals=heads * keys * tokens,
        ),
    )(mask, first, queries, grad_attn, keys_values, keys_values, cos_t, sin_t)


def rotate(values, cosine, sine):
    rows = values.shape[0]
    pieces = values.reshape(rows, -1, HEAD)
    low, high = pieces[:, :, :HALF], pieces[:, :, HALF:]
    c, s = cosine[:, None, :], sine[:, None, :]
    return jnp.concatenate([low * c - high * s, high * c + low * s], axis=2).reshape(rows, -1)


def body(devices, groups, normed, w_query, w_key, w_value, positions, block_mask, grad_attn):
    tokens, width = normed.shape
    kv_cols = w_key.shape[1]
    kv_local = kv_cols // HEAD
    q_cols = w_query.shape[1]
    me = lax.axis_index("seq")
    part = width // devices // groups
    my_part = lax.dynamic_slice_in_dim(
        normed.reshape(tokens, devices, groups * part), lax.axis_index("kvh") * part, part, 2
    )
    columns = lax.all_to_all(
        my_part.reshape(tokens, devices * part), "seq", split_axis=1, concat_axis=0, tiled=True
    )
    columns = lax.all_gather(columns, "kvh", axis=1, tiled=True)

    frequency = THETA ** (-(jnp.arange(HALF, dtype=jnp.float32) * (2.0 / HEAD)))
    angles = positions.astype(jnp.float32)[:, None] * frequency[None, :]
    cosine, sine = jnp.cos(angles), jnp.sin(angles)

    def project(weight):
        return jnp.dot(normed, weight, preferred_element_type=jnp.float32)

    keys = rotate(project(w_key), cosine, sine).astype(jnp.bfloat16)
    values = project(w_value).astype(jnp.bfloat16)
    queries = rotate(project(w_query), cosine, sine).astype(jnp.bfloat16)
    keys_values = gather(jnp.concatenate([keys, values], axis=1), devices, 1)
    first = (me * (tokens // BLOCK)).astype(jnp.int32).reshape(1)
    dq, dk_part, dv_part = attention(
        queries, grad_attn, keys_values, block_mask, first, cosine.T, sine.T, kv_local
    )
    kv_total = reduce_to_owner(jnp.concatenate([dk_part, dv_part], axis=1), devices, 2)
    dk = rotate(kv_total[:, :kv_cols], cosine, -sine).astype(jnp.bfloat16)
    dv = kv_total[:, kv_cols:].astype(jnp.bfloat16)

    partial = dot(dq, w_query, (1, 1)) + dot(dk, w_key, (1, 1)) + dot(dv, w_value, (1, 1))
    grad_normed = lax.psum_scatter(
        partial.astype(jnp.bfloat16), "kvh", scatter_dimension=1, tiled=True
    )
    joined = gather(jnp.concatenate([dq, dk, dv], axis=1), devices, 3)
    grad_wq = dot(columns, joined[:, :q_cols], (0, 0))
    grad_wk = dot(columns, joined[:, q_cols : q_cols + kv_cols], (0, 0))
    grad_wv = dot(columns, joined[:, q_cols + kv_cols :], (0, 0))
    return (grad_normed, grad_wq, grad_wk, grad_wv)


def solution(mesh):
    in_specs = (
        P("seq", None),
        P(None, "kvh"),
        P(None, "kvh"),
        P(None, "kvh"),
        P("seq"),
        P("seq", None),
        P("seq", "kvh"),
    )
    out_specs = (P("seq", "kvh"),) * 4
    return jax.shard_map(
        functools.partial(body, mesh.shape["seq"], mesh.shape["kvh"]),
        mesh=mesh,
        in_specs=in_specs,
        out_specs=out_specs,
        check_vma=False,
    )
```

time: 326 us -> 216 us (0.66)
  waiting for transfers between devices: 213 us -> 0.1 us
  Pallas kernels: 0 us -> 142 us
  matrix products: 70.6 us -> 29.9 us
  starting transfers between devices: 0.25 us -> 6.4 us
  local copies, waits for them, and re-layouts: 18.6 us -> 13.1 us
    reduce_scatter x4 -> x1, waiting for transfers between devices: 190 us -> 0.01 us  [body(): lax.psum_scatter(partial.astype(jnp.bfloat16), 'kvh', scatter_dimension=1...]
    pallas_call x0 -> x4, Pallas kernels: none -> 142 us  [the longest x2 90 us: gather(): pl.pallas_call(functools.partial(gather_kernel, chips), out_shape=jax.Sha...]
    dot_general x18 -> x9, matrix products: 63.8 us -> 29.9 us  [the longest x6 19.6 us: dot(): lax.dot_general(left, right, ((contract[:1], contract[1:]), ((), ())), pr...]
    all_gather x2 -> x1, waiting for transfers between devices: 23.2 us -> 0.02 us  [body(): columns = lax.all_gather(columns, 'kvh', axis=1, tiled=True)]
    reshape x1 -> x0, matrix products: 6.8 us -> none  [rotate(): pieces = values.reshape(tok_rows, head_count, HEAD)]
    all_to_all x0 -> x1, starting transfers between devices: none -> 6.33 us  [body(): lax.all_to_all(my_part.reshape(tokens, devices * part), 'seq', split_axis...]
    unnamed x38 -> x35, local copies, waits for them, and re-layouts: 12.9 us -> 9.05 us
    slice x4 -> x3, local copies, waits for them, and re-layouts: 4.78 us -> 1.01 us  [the longest x1 0.97 us: body(): dk = rotate(kv_total[:, :kv_cols], cosine, -sine).astype(jnp.bfloat16)]
  transfers between devices with their start and end apart: 6 -> 3, of which waited for: 6 -> 0; matrix products, arithmetic and copies ran while one was open for 19% -> 20% of each run, Pallas kernels for 0% -> 66%
where the time goes in v1:
time: 216 us
  Pallas kernels  142 us (66%)
  matrix products  29.9 us (14%)
  between operations  14.3 us (7%)
  local copies, waits for them, and re-layouts  13.1 us (6%)
  other arithmetic  9.8 us (5%)
  starting transfers between devices  6.4 us (3%)
    pallas_call x2, Pallas kernels, gather(): pl.pallas_call(functools.partial(gather_kernel, chips), out_shape=jax.Sha...  90 us
    pallas_call x1, Pallas kernels, attention(): pl.pallas_call(functools.partial(attention_kernel, group, 512), grid=(hea...  26.4 us
    pallas_call x1, Pallas kernels, reduce_to_owner(): pl.pallas_call(functools.partial(reduce_kernel, chips), out_shape=jax.Sha...  25.6 us
    dot_general x6, matrix products, dot(): lax.dot_general(left, right, ((contract[:1], contract[1:]), ((), ())), pr...  19.6 us
    dot_general x3, matrix products, project(): return jnp.dot(normed, weight, preferred_element_type=jnp.float32)  10.3 us
    unnamed x35, local copies, waits for them, and re-layouts  9.05 us
    all_to_all x1, starting transfers between devices, body(): lax.all_to_all(my_part.reshape(tokens, devices * part), 'seq', split_axis...  6.33 us
  transfers between devices with their start and end apart: 3, of which 0 were waited for; matrix products, arithmetic and copies ran while one was open for 20% of the time, Pallas kernels for 66%

profile of v1, /device:TPU:0, one launch (start us, length us, event | category | flops | bytes accessed | tf_op | source)
XLA Modules:
  0.0 215.6 jit_solution(17040841166261849008)
XLA Ops:
  7.2 0.0 copy-start
  7.2 4.2 %copy.20 = bf16[256,4096]{0,1:T(8,128)(2,1)} copy(bf16[256,4096]{1,0:T(8,128)(2,1)} %param.7) | data formatting | bytes 4194304 | tf_op args[0]
  11.4 0.0 copy-start.12
  11.4 1.9 constant_dynamic-slice_fusion
  13.3 6.3 %all-to-all-start = ((bf16[256,8,128]{0,2,1:T(8,128)(2,1)}), bf16[256,8,128]{0,2,1:T(8,128)(2,1)S(1)}, u32[]{:S(2)}, u32[]{:S(2)}) async-start(bf16[256,8,128]{0,2,1:T(8,128)(2,1)} %constant_dynamic-slice_fusion), calls=%async_computation.1 | async-start | bytes 1048576 | tf_op jit(solution)/shard_map/all_to_all | solution.py:355
  19.6 0.0 all-gather.2.cloned.1.call-start
  19.7 0.0 copy-done.12
  19.7 0.0 copy-done
  19.7 2.5 %fusion.10 = f32[256,256]{0,1:T(8,128)S(1)} fusion(bf16[256,4096]{1,0:T(8,128)(2,1)} %param.7, bf16[4096,256]{1,0:T(8,128)(2,1)S(1)} %copy-done), kind=kOutput, calls=%fused_computation.36 | convolution fusion | flops 536870912 | bytes 4456448 | tf_op jit(solution)/shard_map/dot_general | solution.py:365
  22.3 0.1 copy.24
  22.4 0.8 copy.23
  23.3 6.3 %convolution_bitcast_fusion = f32[32,8,8,128]{3,1,2,0:T(8,128)S(1)} fusion(bf16[256,4096]{1,0:T(8,128)(2,1)} %param.7, bf16[4096,1024]{1,0:T(8,128)(2,1)} %param.8), kind=kOutput, calls=%fused_computation.6 | convolution fusion | flops 2147483648 | bytes 11534336 | tf_op jit(solution)/shard_map/dot_general | solution.py:365
  29.6 0.2 copy.25
  29.8 1.2 fusion.7
  31.0 0.0 copy-start.6
  31.0 0.0 copy-start.4
  31.0 0.5 subtract_convert_fusion
  31.5 0.0 copy-start.1
  31.5 0.3 pad_maximum_fusion.2
  31.8 0.1 copy-done.6
  32.0 1.0 subtract_convert_fusion.2
  32.9 0.0 copy-done.4
  33.0 0.6 copy-done.1
  33.5 0.0 copy-start.8
  33.5 0.0 copy-start.9
  33.5 1.4 convolution_convert_fusion
  34.9 0.0 all-to-all-done
  35.0 1.0 copy.21
  36.0 0.0 all-gather.2.cloned.1.call-update
  36.0 0.0 reduce-scatter.2.cloned.1.call-start
  36.1 0.0 copy-done.8
  36.1 0.0 copy-done.9
  36.1 0.4 pad_maximum_fusion.4
  36.5 0.9 copy.33
  37.4 0.0 copy-done.11
  37.4 0.7 pad_maximum_fusion.3.own
  38.1 25.7 %shard_map.102 = bf16[8,256,512]{2,1,0:T(8,128)(2,1)} custom-call(bf16[256,512]{1,0:T(8,128)(2,1)} %pad_maximum_fusion.3.own), custom_call_target="tpu_custom_call" | custom-call | bytes 25165824 | tf_op jit(solution)/shard_map/pallas_call | solution.py:120
  63.8 1.0 multiply_sine_fusion.1
  64.8 26.4 %shard_map.103 = (bf16[256,1024]{1,0:T(8,128)(2,1)}, bf16[2048,256]{1,0:T(8,128)(2,1)}, bf16[2048,256]{1,0:T(8,128)(2,1)}) custom-call(s32[2,16]{1,0:T(2,128)} %mask.1, s32[1]{0:T(128)} %bitcast.first, bf16[256,1024]{1,0:T(8,128)(2,1)} %bitcast.53, bf16[256,1024]{1,0:T(8,128)(2,1)} %g.1, bf16[2048,512]{1,0:T(8,128)(2,1)} %bitcast.44, ...), custom_call_target="tpu_custom_call" | custom-call | flops 5368709120 | bytes 4194304 | tf_op jit(solution)/shard_map/pallas_call | solution.py:296
  91.2 3.0 %pad_maximum_fusion = bf16[2048,512]{1,0:T(8,128)(2,1)} fusion(bf16[2048,256]{1,0:T(8,128)(2,1)} %get-tuple-element.9, bf16[2048,256]{1,0:T(8,128)(2,1)} %get-tuple-element.8), kind=kLoop, calls=%fused_computation.5 | loop fusion | flops 4194304 | bytes 4194304 | tf_op jit(solution)/shard_map/concatenate | solution.py:375
  94.2 25.6 %shard_map.104 = f32[256,512]{1,0:T(8,128)} custom-call(bf16[8,256,512]{2,1,0:T(8,128)(2,1)} %bitcast.38), custom_call_target="tpu_custom_call" | custom-call | bytes 25165824 | tf_op jit(solution)/shard_map/pallas_call | solution.py:201
  119.9 1.0 slice.38
  120.8 0.1 reshape.120
  121.0 0.0 copy-done.10
  121.0 0.5 subtract_convert_fusion.1
  121.5 0.4 pad_maximum_fusion.5
  121.8 5.9 %fusion.11 = f32[256,4096]{1,0:T(8,128)S(1)} fusion(bf16[256,1024]{1,0:T(8,128)(2,1)} %get-tuple-element.7, bf16[4096,1024]{1,0:T(8,128)(2,1)} %param.8), kind=kOutput, calls=%fused_computation.37 | convolution fusion | flops 2147483648 | bytes 13107200 | tf_op jit(solution)/shard_map/dot_general | solution.py:215
  127.8 0.0 copy-start.3
  127.8 0.0 copy-start.5
  127.8 0.7 convolution_add_fusion.1
  128.6 0.3 copy-done.3
  128.8 0.7 copy-done.5
  129.6 2.2 fusion
  131.7 0.0 reduce-scatter.2.cloned.1.call-update
  131.8 1.0 copy-done.7
  132.7 0.9 pad_maximum_fusion.1.own
  133.7 64.3 %shard_map.105 = bf16[8,256,1536]{2,1,0:T(8,128)(2,1)} custom-call(bf16[256,1536]{1,0:T(8,128)(2,1)} %pad_maximum_fusion.1.own), custom_call_target="tpu_custom_call" | custom-call | bytes 75497472 | tf_op jit(solution)/shard_map/pallas_call | solution.py:120
  198.0 0.0 all-gather.2.cloned.1.call-done
  198.0 0.0 copy-start.2
  198.0 3.5 %fusion.3 = f32[512,256]{1,0:T(8,128)} fusion(bf16[2048,512]{1,0:T(8,128)(2,1)} %all-gather.2.cloned.1.call-done, bf16[2048,1536]{1,0:T(8,128)(2,1)} %bitcast.39), kind=kOutput, calls=%fused_computation.8 | convolution fusion | flops 536870912 | bytes 3670016 | tf_op jit(solution)/shard_map/dot_general | solution.py:215
  201.6 3.5 %fusion.5 = f32[512,256]{1,0:T(8,128)} fusion(bf16[2048,512]{1,0:T(8,128)(2,1)} %all-gather.2.cloned.1.call-done, bf16[2048,1536]{1,0:T(8,128)(2,1)} %bitcast.40), kind=kOutput, calls=%fused_computation.10 | convolution fusion | flops 536870912 | bytes 3670016 | tf_op jit(solution)/shard_map/dot_general | solution.py:215
  205.1 0.0 copy-done.2
  205.1 0.0 copy-done.13
  205.1 3.7 %fusion.1 = f32[512,1024]{1,0:T(8,128)} fusion(bf16[2048,512]{1,0:T(8,128)(2,1)S(1)} %copy-done.13, bf16[2048,1536]{1,0:T(8,128)(2,1)S(1)} %bitcast.41), kind=kOutput, calls=%fused_computation.3 | convolution fusion | flops 2147483648 | bytes 8388608 | tf_op jit(solution)/shard_map/dot_general | solution.py:215
  (11 shorter events, 0.1 us)
Async XLA Ops:
  7.2 12.5 %copy-start = (bf16[4096,256]{1,0:T(8,128)(2,1)S(1)}, bf16[4096,256]{1,0:T(8,128)(2,1)}, u32[]{:S(2)}) copy-start(bf16[4096,256]{1,0:T(8,128)(2,1)} %param.9) | copy-start | bytes 6291460
  11.4 8.3 %copy-start.12 = (s32[256]{0:T(256)S(1)}, s32[256]{0:T(256)}, u32[]{:S(2)}) copy-start(s32[256]{0:T(256)} %param.11) | copy-start | bytes 3076
  13.3 21.7 %all-to-all-start = ((bf16[256,8,128]{0,2,1:T(8,128)(2,1)}), bf16[256,8,128]{0,2,1:T(8,128)(2,1)S(1)}, u32[]{:S(2)}, u32[]{:S(2)}) async-start(bf16[256,8,128]{0,2,1:T(8,128)(2,1)} %constant_dynamic-slice_fusion), calls=%async_computation.1 | async-start | bytes 1048576 | tf_op jit(solution)/shard_map/all_to_all | solution.py:355
  19.6 178.4 %all-gather.2.cloned.1.call-start = ((), (), s32[]{:S(2)}) async-start(), calls=%async_computation.3 | async-start | bytes 2621440 | tf_op jit(solution)/shard_map/all_gather | solution.py:358
  31.0 0.9 copy-start.6
  31.0 1.9 copy-start.4
  31.5 2.0 copy-start.1
  33.5 2.5 %copy-start.8 = (bf16[256,2,64]{2,1,0:T(2,128)(2,1)S(1)}, bf16[256,2,64]{2,1,0:T(2,128)(2,1)}, u32[]{:S(2)}) copy-start(bf16[256,2,64]{2,1,0:T(2,128)(2,1)} %get-tuple-element.12) | copy-start | bytes 196612
  33.5 2.5 %copy-start.9 = (bf16[256,2,64]{2,1,0:T(2,128)(2,1)S(1)}, bf16[256,2,64]{2,1,0:T(2,128)(2,1)}, u32[]{:S(2)}) copy-start(bf16[256,2,64]{2,1,0:T(2,128)(2,1)} %get-tuple-element.13) | copy-start | bytes 196612
  36.0 1.4 copy-start.11
  36.0 172.8 %reduce-scatter.2.cloned.1.call-start = ((), (), s32[]{:S(2)}) async-start(), calls=%async_computation.2 | async-start | bytes 2621440 | tf_op jit(solution)/shard_map/reduce_scatter | solution.py:380
  94.2 26.8 %copy-start.10 = (f32[256,64]{1,0:T(8,128)S(1)}, f32[256,64]{1,0:T(8,128)}, u32[]{:S(2)}) copy-start(f32[256,64]{1,0:T(8,128)} %get-tuple-element.18) | copy-start | bytes 196612
  127.8 1.0 copy-start.3
  127.8 1.8 copy-start.5
  131.7 1.0 copy-start.7
  198.0 7.1 %copy-start.2 = (bf16[8,256,1536]{2,1,0:T(8,128)(2,1)S(1)}, bf16[8,256,1536]{2,1,0:T(8,128)(2,1)}, u32[]{:S(2)}) copy-start(bf16[8,256,1536]{2,1,0:T(8,128)(2,1)} %shard_map.105) | copy-start | bytes 18874372
  201.6 3.6 %copy-start.13 = (bf16[2048,512]{1,0:T(8,128)(2,1)S(1)}, bf16[2048,512]{1,0:T(8,128)(2,1)}, u32[]{:S(2)}) copy-start(bf16[2048,512]{1,0:T(8,128)(2,1)} %all-gather.2.cloned.1.call-done) | copy-start | bytes 6291460
Sparse Core Ops, SparseCore 0:
  36.1 36.5 all-gather.1
  131.8 39.1 reduce-scatter.1

commit v2 on v1

--- a/solution.py
+++ b/solution.py
@@ -218,11 +218,105 @@
 
 
 def attention_kernel(
-    group, chunk, mask, first, q, g, k, v, cos_t, sin_t, dq, dk, dv, bias, scores, gprobs, weights,
-    k_t, dk_sum, dv_sum
+    group, chunk, chips, pairs, mask, first, q, g, k, v, cos_t, sin_t, own, out, dkv, bias, scores,
+    gprobs, weights, k_t, dk_sum, dv_sum, local_sem, send_r, send_l, send_p, recv_l, recv_r, recv_p
 ):
     step = pl.program_id(0)
     keys, tokens = bias.shape
+    wide = 2 * HEAD
+    me = lax.axis_index("seq")
+    chip, core = me // 2, me % 2
+    other = chip * 2 + 1 - core
+    has_left, has_right = chip > 0, chip < chips - 1
+
+    @pl.when(step == 0)
+    def _():
+        barrier = pltpu.get_barrier_semaphore()
+
+        def greet(device):
+            pl.semaphore_signal(barrier, inc=1, device_id={"seq": device}, device_id_type=MESH)
+
+        greet(other)
+        pl.when(has_left)(lambda: greet(me - 2))
+        pl.when(has_right)(lambda: greet(me + 2))
+        pl.semaphore_wait(barrier, 1 + has_left.astype(jnp.int32) + has_right.astype(jnp.int32))
+
+    def columns_of(pair):
+        start = pair * wide
+        return pl.ds(start if isinstance(pair, int) else pl.multiple_of(start, wide), wide)
+
+    def place(slot, pair):
+        return out.at[slot, :, columns_of(pair)]
+
+    def remote(pair, offset, send, recv, device):
+        slot = me + 2 * offset
+        return pltpu.make_async_remote_copy(
+            src_ref=own.at[:, columns_of(pair)] if offset == 0 else place(slot, pair),
+            dst_ref=place(slot, pair),
+            send_sem=send,
+            recv_sem=recv,
+            device_id={"seq": device},
+            device_id_type=MESH,
+        )
+
+    def right(pair, t):
+        return remote(pair, -t, send_r.at[pair, t], recv_l.at[pair, t + 1], me + 2)
+
+    def left(pair, t):
+        return remote(pair, t, send_l.at[pair, t], recv_r.at[pair, t + 1], me - 2)
+
+    def partner(pair, offset):
+        at = offset + chips - 1
+        return remote(pair, offset, send_p.at[pair, at], recv_p.at[pair, at], other)
+
+    def arrival(slot, pair, sem):
+        pltpu.make_async_copy(place(slot, pair), place(slot, pair), sem).wait()
+
+    def stay(pair):
+        return pltpu.make_async_copy(
+            own.at[:, columns_of(pair)], place(me, pair), local_sem.at[pair]
+        )
+
+    def begin(pair):
+        pl.when(has_right)(lambda: right(pair, 0).start())
+        pl.when(has_left)(lambda: left(pair, 0).start())
+        partner(pair, 0).start()
+        stay(pair).start()
+
+    def forward(pair, t):
+        @pl.when(chip - t >= 0)
+        def _():
+            arrival(me - 2 * t, pair, recv_l.at[pair, t])
+            if t < chips - 1:
+                pl.when(has_right)(lambda: right(pair, t).start())
+            partner(pair, -t).start()
+
+        @pl.when(chip + t < chips)
+        def _():
+            arrival(me + 2 * t, pair, recv_r.at[pair, t])
+            if t < chips - 1:
+                pl.when(has_left)(lambda: left(pair, t).start())
+            partner(pair, t).start()
+
+    def finish(pair):
+        stay(pair).wait()
+        for t in range(chips):
+
+            @pl.when(chip - t >= 0)
+            def _():
+                arrival(other - 2 * t, pair, recv_p.at[pair, chips - 1 - t])
+                partner(pair, -t).wait_send()
+                if t < chips - 1:
+                    pl.when(has_right)(lambda: right(pair, t).wait_send())
+
+            @pl.when(chip + t < chips)
+            def _():
+                if t > 0:
+                    arrival(other + 2 * t, pair, recv_p.at[pair, chips - 1 + t])
+                    partner(pair, t).wait_send()
+                if t < chips - 1:
+                    pl.when(has_left)(lambda: left(pair, t).wait_send())
+
     chunks = [pl.ds(c * chunk, chunk) for c in range(keys // chunk)]
 
     @pl.when(step == 0)
@@ -276,30 +370,50 @@
     low, high = dq_t[:HALF, :], dq_t[HALF:, :]
     c, s = cos_t[...], sin_t[...]
     turned = jnp.concatenate([low * c + high * s, high * c - low * s], axis=0)
-    dq[...] = turned.T.astype(jnp.bfloat16)
+    own[:, pl.ds(pl.multiple_of(step * HEAD, HEAD), HEAD)] = turned.T.astype(jnp.bfloat16)
 
     @pl.when(step % group == group - 1)
     def _():
-        dk[...] = dk_sum[...].astype(jnp.bfloat16)
-        dv[...] = dv_sum[...].astype(jnp.bfloat16)
-
-
-def attention(queries, grad_attn, keys_values, mask, first, cos_t, sin_t, kv_local):
+        head = step // group
+        dkv[:, pl.ds(pl.multiple_of(head * HEAD, HEAD), HEAD)] = dk_sum[...].astype(jnp.bfloat16)
+        at = pl.multiple_of(dkv.shape[1] // 2 + head * HEAD, HEAD)
+        dkv[:, pl.ds(at, HEAD)] = dv_sum[...].astype(jnp.bfloat16)
+
+    @pl.when(step % 2 == 1)
+    def _():
+        pair = step // 2
+        begin(pair)
+        for t in range(1, min(chips, pairs)):
+            pl.when(pair - t >= 0)(lambda: forward(pair - t, t))
+
+    @pl.when(step == 2 * pairs - 1)
+    def _():
+        for at in range(pairs, pairs + chips - 1):
+            for t in range(1, chips):
+                if at - t < pairs and at - t >= 0:
+                    forward(at - t, t)
+        for pair in range(pairs):
+            finish(pair)
+
+
+def attention(queries, grad_attn, keys_values, mask, first, cos_t, sin_t, kv_local, devices):
     tokens = queries.shape[0]
     heads = queries.shape[1] // HEAD
     group = heads // kv_local
     keys = keys_values.shape[0]
     f32, bf16 = jnp.float32, jnp.bfloat16
+    chips, pairs = devices // 2, heads // 2
+    dma = pltpu.SemaphoreType.DMA
     one_head = pl.BlockSpec((tokens, HEAD), lambda h: (0, h))
     angle = pl.BlockSpec((HALF, tokens), lambda h: (0, 0))
     smem = pl.BlockSpec(memory_space=pltpu.SMEM)
     return pl.pallas_call(
-        functools.partial(attention_kernel, group, 512),
+        functools.partial(attention_kernel, group, 512, chips, pairs),
         grid=(heads,),
         out_shape=[
             jax.ShapeDtypeStruct((tokens, heads * HEAD), bf16),
-            jax.ShapeDtypeStruct((keys, kv_local * HEAD), bf16),
-            jax.ShapeDtypeStruct((keys, kv_local * HEAD), bf16),
+            jax.ShapeDtypeStruct((devices, tokens, heads * HEAD), bf16),
+            jax.ShapeDtypeStruct((keys, 2 * kv_local * HEAD), bf16),
         ],
         in_specs=[
             smem,
@@ -312,9 +426,9 @@
             angle,
         ],
         out_specs=[
-            one_head,
-            pl.BlockSpec((keys, HEAD), lambda h: (0, h // group)),
-            pl.BlockSpec((keys, HEAD), lambda h: (0, h // group)),
+            pl.BlockSpec((tokens, heads * HEAD), lambda h: (0, 0)),
+            ANY,
+            pl.BlockSpec((keys, 2 * kv_local * HEAD), lambda h: (0, 0)),
         ],
         scratch_shapes=[
             pltpu.VMEM((keys, tokens), f32),
@@ -324,8 +438,15 @@
             pltpu.VMEM((HEAD, keys), bf16),
             pltpu.VMEM((keys, HEAD), f32),
             pltpu.VMEM((keys, HEAD), f32),
+            dma((pairs,)),
+            dma((pairs, chips)),
+            dma((pairs, chips)),
+            dma((pairs, 2 * chips)),
+            dma((pairs, chips + 1)),
+            dma((pairs, chips + 1)),
+            dma((pairs, 2 * chips)),
         ],
-        compiler_params=params(None, ("arbitrary",)),
+        compiler_params=params(4, ("arbitrary",)),
         cost_estimate=pl.CostEstimate(
             flops=10 * keys * tokens * heads * HEAD,
             bytes_accessed=8 * keys * HEAD * kv_local,
@@ -349,11 +470,12 @@
     q_cols = w_query.shape[1]
     me = lax.axis_index("seq")
     part = width // devices // groups
-    my_part = lax.dynamic_slice_in_dim(
-        normed.reshape(tokens, devices, groups * part), lax.axis_index("kvh") * part, part, 2
-    )
+    at = lax.axis_index("kvh") * part
+    pieces = [
+        lax.dynamic_slice_in_dim(normed, d * groups * part + at, part, 1) for d in range(devices)
+    ]
     columns = lax.all_to_all(
-        my_part.reshape(tokens, devices * part), "seq", split_axis=1, concat_axis=0, tiled=True
+        jnp.concatenate(pieces, axis=0), "seq", split_axis=0, concat_axis=0, tiled=True
     )
     columns = lax.all_gather(columns, "kvh", axis=1, tiled=True)
 
@@ -369,10 +491,11 @@
     queries = rotate(project(w_query), cosine, sine).astype(jnp.bfloat16)
     keys_values = gather(jnp.concatenate([keys, values], axis=1), devices, 1)
     first = (me * (tokens // BLOCK)).astype(jnp.int32).reshape(1)
-    dq, dk_part, dv_part = attention(
-        queries, grad_attn, keys_values, block_mask, first, cosine.T, sine.T, kv_local
+    dq, dq_all, dkv_part = attention(
+        queries, grad_attn, keys_values, block_mask, first, cosine.T, sine.T, kv_local, devices
     )
-    kv_total = reduce_to_owner(jnp.concatenate([dk_part, dv_part], axis=1), devices, 2)
+    dq_all = dq_all.reshape(devices * tokens, q_cols)
+    kv_total = reduce_to_owner(dkv_part, devices, 2)
     dk = rotate(kv_total[:, :kv_cols], cosine, -sine).astype(jnp.bfloat16)
     dv = kv_total[:, kv_cols:].astype(jnp.bfloat16)
 
@@ -380,10 +503,10 @@
     grad_normed = lax.psum_scatter(
         partial.astype(jnp.bfloat16), "kvh", scatter_dimension=1, tiled=True
     )
-    joined = gather(jnp.concatenate([dq, dk, dv], axis=1), devices, 3)
-    grad_wq = dot(columns, joined[:, :q_cols], (0, 0))
-    grad_wk = dot(columns, joined[:, q_cols : q_cols + kv_cols], (0, 0))
-    grad_wv = dot(columns, joined[:, q_cols + kv_cols :], (0, 0))
+    dkv_all = gather(jnp.concatenate([dk, dv], axis=1), devices, 3)
+    grad_wq = dot(columns, dq_all, (0, 0))
+    grad_wk = dot(columns, dkv_all[:, :kv_cols], (0, 0))
+    grad_wv = dot(columns, dkv_all[:, kv_cols:], (0, 0))
     return (grad_normed, grad_wq, grad_wk, grad_wv)
 
 

time: 216 us -> 209 us (0.968)
  Pallas kernels: 142 us -> 133 us
  local copies, waits for them, and re-layouts: 13.1 us -> 18.2 us
  other arithmetic: 9.8 us -> 5.88 us
  waiting for transfers between devices: 0.1 us -> 2.82 us
  matrix products: 29.9 us -> 27.6 us
    pallas_call x2, Pallas kernels: 90 us -> 54.7 us  [gather(): pl.pallas_call(functools.partial(gather_kernel, chips), out_shape=jax.Sha...]
    pallas_call x1, Pallas kernels: 26.4 us -> 52.4 us  [attention(): pl.pallas_call(functools.partial(attention_kernel, group, 512, chips, pai...]
    unnamed x35, local copies, waits for them, and re-layouts: 9.05 us -> 15.6 us
    concatenate x2 -> x1, other arithmetic: 3.94 us -> 0.72 us  [body(): dkv_all = gather(jnp.concatenate([dk, dv], axis=1), devices, 3)]
    all_to_all x1, waiting for transfers between devices: 0.04 us -> 2.77 us  [body(): lax.all_to_all(jnp.concatenate(pieces, axis=0), 'seq', split_axis=0, conc...]
    dot_general x6, matrix products: 19.6 us -> 17.4 us  [dot(): lax.dot_general(left, right, ((contract[:1], contract[1:]), ((), ())), pr...]
  transfers between devices with their start and end apart: 3 -> 3, of which waited for: 0 -> 1; matrix products, arithmetic and copies ran while one was open for 20% -> 17% of each run, Pallas kernels for 66% -> 64%
where the time goes in v2:
time: 209 us; the launch traced here: 208 us
  Pallas kernels  133 us (64%)
  matrix products  27.6 us (13%)
  local copies, waits for them, and re-layouts  18.2 us (9%)
  between operations  14.3 us (7%)
  starting transfers between devices  6.4 us (3%)
  other arithmetic  5.88 us (3%)
  waiting for transfers between devices  2.82 us (1%)
    pallas_call x2, Pallas kernels, gather(): pl.pallas_call(functools.partial(gather_kernel, chips), out_shape=jax.Sha...  54.7 us
    pallas_call x1, Pallas kernels, attention(): pl.pallas_call(functools.partial(attention_kernel, group, 512, chips, pai...  52.4 us
    pallas_call x1, Pallas kernels, reduce_to_owner(): pl.pallas_call(functools.partial(reduce_kernel, chips), out_shape=jax.Sha...  26 us
    dot_general x6, matrix products, dot(): lax.dot_general(left, right, ((contract[:1], contract[1:]), ((), ())), pr...  17.4 us
    unnamed x35, local copies, waits for them, and re-layouts  15.6 us
    dot_general x3, matrix products, project(): return jnp.dot(normed, weight, preferred_element_type=jnp.float32)  10.3 us
    all_to_all x1, starting transfers between devices, body(): lax.all_to_all(jnp.concatenate(pieces, axis=0), 'seq', split_axis=0, conc...  6.33 us
  transfers between devices with their start and end apart: 3, of which 1 were waited for; matrix products, arithmetic and copies ran while one was open for 17% of the time, Pallas kernels for 64%

profile of v2, /device:TPU:0, one launch (start us, length us, event | category | flops | bytes accessed | tf_op | source)
XLA Modules:
  0.0 208.4 jit_solution(17212280317811089372)
XLA Ops:
  7.2 0.0 copy-start
  7.2 1.6 dynamic-slice_dynamic-update-slice_fusion.7
  8.8 1.5 dynamic-slice_dynamic-update-slice_fusion.6
  10.3 1.5 dynamic-slice_dynamic-update-slice_fusion.5
  11.8 1.5 dynamic-slice_dynamic-update-slice_fusion.4
  13.2 1.5 dynamic-slice_dynamic-update-slice_fusion.3
  14.7 1.5 dynamic-slice_dynamic-update-slice_fusion.2
  16.2 1.5 dynamic-slice_dynamic-update-slice_fusion.1
  17.6 1.5 dynamic-slice_dynamic-update-slice_fusion
  19.1 6.3 %all-to-all-start = ((bf16[8,256,128]{2,1,0:T(8,128)(2,1)}), bf16[8,256,128]{2,1,0:T(8,128)(2,1)S(1)}, u32[]{:S(2)}, u32[]{:S(2)}) async-start(bf16[8,256,128]{2,1,0:T(8,128)(2,1)} %bitcast.4), calls=%async_computation.1 | async-start | bytes 1048576 | tf_op jit(solution)/shard_map/all_to_all | solution.py:477
  25.4 0.0 all-gather.2.cloned.1.call-start
  25.5 6.3 %convolution_bitcast_fusion = f32[32,8,8,128]{3,1,2,0:T(8,128)S(1)} fusion(bf16[256,4096]{1,0:T(8,128)(2,1)} %param.7, bf16[4096,1024]{1,0:T(8,128)(2,1)} %param.8), kind=kOutput, calls=%fused_computation.3 | convolution fusion | flops 2147483648 | bytes 11534336 | tf_op jit(solution)/shard_map/dot_general | solution.py:487
  31.9 0.0 copy-start.7
  31.9 0.2 copy.17
  32.1 0.5 copy-done.7
  32.5 1.2 fusion.5
  33.7 0.5 subtract_convert_fusion
  34.3 0.0 copy-start.1
  34.3 0.3 pad_maximum_fusion
  34.6 0.9 copy.25
  35.5 0.0 copy-done
  35.5 0.6 copy-done.1
  36.0 1.0 fusion.8
  37.0 0.1 copy.16
  37.2 0.1 copy.15
  37.4 0.3 subtract_convert_fusion.2
  37.6 0.4 pad_maximum_fusion.3
  38.0 2.8 %all-to-all-done = bf16[8,256,128]{2,1,0:T(8,128)(2,1)S(1)} async-done(((bf16[8,256,128]{2,1,0:T(8,128)(2,1)}), bf16[8,256,128]{2,1,0:T(8,128)(2,1)S(1)}, u32[]{:S(2)}, u32[]{:S(2)}) %all-to-all-start) | async-done | bytes 524320 | tf_op jit(solution)/shard_map/all_to_all | solution.py:477
  40.8 0.8 copy-done.4
  41.6 0.0 all-gather.2.cloned.1.call-update
  41.6 0.0 reduce-scatter.2.cloned.1.call-start
  41.7 2.9 %convolution_convert_fusion = bf16[256,256]{1,0:T(8,128)(2,1)S(1)} fusion(bf16[256,4096]{1,0:T(8,128)(2,1)} %param.7, bf16[4096,256]{1,0:T(8,128)(2,1)} %param.10), kind=kOutput, calls=%fused_computation.4 | convolution fusion | flops 536936448 | bytes 4325376 | tf_op jit(solution)/shard_map/dot_general | solution.py:487
  44.6 0.7 pad_maximum_fusion.1.own
  45.3 23.5 %shard_map.102 = bf16[8,256,512]{2,1,0:T(8,128)(2,1)} custom-call(bf16[256,512]{1,0:T(8,128)(2,1)} %pad_maximum_fusion.1.own), custom_call_target="tpu_custom_call" | custom-call | bytes 25165824 | tf_op jit(solution)/shard_map/pallas_call | solution.py:120
  68.8 1.0 multiply_sine_fusion.1
  69.8 52.4 %shard_map.103 = (bf16[256,1024]{1,0:T(8,128)(2,1)}, bf16[8,256,1024]{2,1,0:T(8,128)(2,1)}, bf16[2048,512]{1,0:T(8,128)(2,1)}) custom-call(s32[2,16]{1,0:T(2,128)} %mask.1, s32[1]{0:T(128)} %bitcast.first, bf16[256,1024]{1,0:T(8,128)(2,1)} %bitcast.50, bf16[256,1024]{1,0:T(8,128)(2,1)} %g.1, bf16[2048,512]{1,0:T(8,128)(2,1)} %bitcast.41, ...), custom_call_target="tpu_custom_call" | custom-call | flops 5368709120 | bytes 4194304 | tf_op jit(solution)/shard_map/pallas_call | solution.py:410
  122.2 0.0 copy-start.6
  122.2 0.0 copy-start.10
  122.2 26.0 %shard_map.104 = f32[256,512]{1,0:T(8,128)} custom-call(bf16[8,256,512]{2,1,0:T(8,128)(2,1)} %bitcast.39), custom_call_target="tpu_custom_call" | custom-call | bytes 25165824 | tf_op jit(solution)/shard_map/pallas_call | solution.py:201
  148.2 1.0 slice.35
  149.1 0.1 reshape.117
  149.3 0.0 copy-done.6
  149.3 0.5 subtract_convert_fusion.1
  149.8 0.4 pad_maximum_fusion.4
  150.1 0.0 copy-done.10
  150.2 5.7 %fusion.9 = f32[256,4096]{1,0:T(8,128)S(1)} fusion(bf16[256,1024]{1,0:T(8,128)(2,1)S(1)} %copy-done.10, bf16[4096,1024]{1,0:T(8,128)(2,1)} %param.8), kind=kOutput, calls=%fused_computation.41 | convolution fusion | flops 2147483648 | bytes 13107200 | tf_op jit(solution)/shard_map/dot_general | solution.py:215
  155.9 0.0 copy-start.2
  155.9 0.0 copy-start.5
  155.9 0.7 convolution_add_fusion.1
  156.7 0.3 copy-done.2
  157.0 0.7 copy-done.5
  157.7 2.1 %fusion = bf16[256,4096]{1,0:T(8,128)(2,1)} fusion(f32[256,4096]{1,0:T(8,128)S(1)} %convolution_add_fusion.1, bf16[4096,256]{1,0:T(8,128)(2,1)S(1)} %copy-done.5, f32[256,512]{1,0:T(8,128)S(1)} %copy-done.2), kind=kOutput, calls=%fused_computation.2 | convolution fusion | flops 538968064 | bytes 8519680 | tf_op jit(solution)/shard_map/dot_general | solution.py:215
  159.8 0.0 reduce-scatter.2.cloned.1.call-update
  159.9 0.7 pad_maximum_fusion.2.own
  160.6 31.2 %shard_map.105 = bf16[8,256,512]{2,1,0:T(8,128)(2,1)} custom-call(bf16[256,512]{1,0:T(8,128)(2,1)} %pad_maximum_fusion.2.own), custom_call_target="tpu_custom_call" | custom-call | bytes 25165824 | tf_op jit(solution)/shard_map/pallas_call | solution.py:120
  191.9 0.0 all-gather.2.cloned.1.call-done
  191.9 0.0 copy-start.3
  191.9 0.0 copy-start.8
  191.9 3.6 %fusion.3 = f32[512,256]{1,0:T(8,128)} fusion(bf16[2048,512]{1,0:T(8,128)(2,1)} %all-gather.2.cloned.1.call-done, bf16[2048,512]{1,0:T(8,128)(2,1)} %bitcast.43), kind=kOutput, calls=%fused_computation.7 | convolution fusion | flops 536870912 | bytes 3670016 | tf_op jit(solution)/shard_map/dot_general | solution.py:215
  195.5 0.0 copy-done.3
  195.5 0.0 copy-done.8
  195.5 1.5 fusion.1
  197.0 0.9 copy-done.9
  197.9 3.7 %fusion.10 = f32[512,1024]{1,0:T(8,128)} fusion(bf16[2048,512]{1,0:T(8,128)(2,1)S(1)} %copy-done.8, bf16[2048,1024]{1,0:T(8,128)(2,1)S(1)} %bitcast.53), kind=kOutput, calls=%fused_computation.42 | convolution fusion | flops 2147483648 | bytes 8388608 | tf_op jit(solution)/shard_map/dot_general | solution.py:215
  (9 shorter events, 0.1 us)
Async XLA Ops:
  7.2 28.3 %copy-start = (bf16[4096,256]{1,0:T(8,128)(2,1)S(1)}, bf16[4096,256]{1,0:T(8,128)(2,1)}, u32[]{:S(2)}) copy-start(bf16[4096,256]{1,0:T(8,128)(2,1)} %param.9) | copy-start | bytes 6291460
  19.1 21.7 %all-to-all-start = ((bf16[8,256,128]{2,1,0:T(8,128)(2,1)}), bf16[8,256,128]{2,1,0:T(8,128)(2,1)S(1)}, u32[]{:S(2)}, u32[]{:S(2)}) async-start(bf16[8,256,128]{2,1,0:T(8,128)(2,1)} %bitcast.4), calls=%async_computation.1 | async-start | bytes 1048576 | tf_op jit(solution)/shard_map/all_to_all | solution.py:477
  25.4 166.4 %all-gather.2.cloned.1.call-start = ((), (), s32[]{:S(2)}) async-start(), calls=%async_computation.3 | async-start | bytes 2621440 | tf_op jit(solution)/shard_map/all_gather | solution.py:480
  31.9 0.7 copy-start.7
  34.3 1.8 copy-start.1
  40.8 0.8 copy-start.4
  41.6 159.9 %reduce-scatter.2.cloned.1.call-start = ((), (), s32[]{:S(2)}) async-start(), calls=%async_computation.2 | async-start | bytes 2621440 | tf_op jit(solution)/shard_map/reduce_scatter | solution.py:503
  122.2 27.1 %copy-start.6 = (f32[256,64]{1,0:T(8,128)S(1)}, f32[256,64]{1,0:T(8,128)}, u32[]{:S(2)}) copy-start(f32[256,64]{1,0:T(8,128)} %get-tuple-element.18) | copy-start | bytes 196612
  122.2 28.0 %copy-start.10 = (bf16[256,1024]{1,0:T(8,128)(2,1)S(1)}, bf16[256,1024]{1,0:T(8,128)(2,1)}, u32[]{:S(2)}) copy-start(bf16[256,1024]{1,0:T(8,128)(2,1)} %get-tuple-element.7) | copy-start | bytes 1572868
  155.9 1.0 copy-start.2
  155.9 1.8 copy-start.5
  191.9 3.6 %copy-start.3 = (bf16[8,256,512]{2,1,0:T(8,128)(2,1)S(1)}, bf16[8,256,512]{2,1,0:T(8,128)(2,1)}, u32[]{:S(2)}) copy-start(bf16[8,256,512]{2,1,0:T(8,128)(2,1)} %shard_map.105) | copy-start | bytes 6291460
  191.9 3.6 %copy-start.8 = (bf16[2048,512]{1,0:T(8,128)(2,1)S(1)}, bf16[2048,512]{1,0:T(8,128)(2,1)}, u32[]{:S(2)}) copy-start(bf16[2048,512]{1,0:T(8,128)(2,1)} %all-gather.2.cloned.1.call-done) | copy-start | bytes 6291460
  195.5 2.4 %copy-start.9 = (bf16[8,256,1024]{2,1,0:T(8,128)(2,1)S(1)}, bf16[8,256,1024]{2,1,0:T(8,128)(2,1)}, u32[]{:S(2)}) copy-start(bf16[8,256,1024]{2,1,0:T(8,128)(2,1)} %get-tuple-element.9) | copy-start | bytes 12582916
Sparse Core Ops, SparseCore 0:
  41.7 34.0 all-gather.1
  160.0 40.9 reduce-scatter.1

commit v3 on v2

--- a/solution.py
+++ b/solution.py
@@ -470,12 +470,11 @@
     q_cols = w_query.shape[1]
     me = lax.axis_index("seq")
     part = width // devices // groups
-    at = lax.axis_index("kvh") * part
-    pieces = [
-        lax.dynamic_slice_in_dim(normed, d * groups * part + at, part, 1) for d in range(devices)
-    ]
+    my_part = lax.dynamic_slice_in_dim(
+        normed.reshape(tokens, devices, groups * part), lax.axis_index("kvh") * part, part, 2
+    )
     columns = lax.all_to_all(
-        jnp.concatenate(pieces, axis=0), "seq", split_axis=0, concat_axis=0, tiled=True
+        my_part.reshape(tokens, devices * part), "seq", split_axis=1, concat_axis=0, tiled=True
     )
     columns = lax.all_gather(columns, "kvh", axis=1, tiled=True)
 

time: 209 us -> 203 us (0.971)
  local copies, waits for them, and re-layouts: 18.2 us -> 12.6 us
    unnamed x35 -> x27, local copies, waits for them, and re-layouts: 15.6 us -> 8.59 us
  transfers between devices with their start and end apart: 3 -> 3, of which waited for: 1 -> 1; matrix products, arithmetic and copies ran while one was open for 17% -> 18% of each run, Pallas kernels for 64% -> 66%
where the time goes in v3:
time: 203 us
  Pallas kernels  133 us (66%)
  matrix products  27.6 us (14%)
  between operations  14.3 us (7%)
  local copies, waits for them, and re-layouts  12.6 us (6%)
  starting transfers between devices  6.4 us (3%)
  other arithmetic  5.89 us (3%)
  waiting for transfers between devices  2.82 us (1%)
    pallas_call x2, Pallas kernels, gather(): pl.pallas_call(functools.partial(gather_kernel, chips), out_shape=jax.Sha...  54.7 us
    pallas_call x1, Pallas kernels, attention(): pl.pallas_call(functools.partial(attention_kernel, group, 512, chips, pai...  52.4 us
    pallas_call x1, Pallas kernels, reduce_to_owner(): pl.pallas_call(functools.partial(reduce_kernel, chips), out_shape=jax.Sha...  26 us
    dot_general x6, matrix products, dot(): lax.dot_general(left, right, ((contract[:1], contract[1:]), ((), ())), pr...  17.4 us
    dot_general x3, matrix products, project(): return jnp.dot(normed, weight, preferred_element_type=jnp.float32)  10.3 us
    unnamed x27, local copies, waits for them, and re-layouts  8.59 us
    all_to_all x1, starting transfers between devices, body(): lax.all_to_all(my_part.reshape(tokens, devices * part), 'seq', split_axis...  6.33 us
  transfers between devices with their start and end apart: 3, of which 1 were waited for; matrix products, arithmetic and copies ran while one was open for 18% of the time, Pallas kernels for 66%

profile of v3, /device:TPU:0, one launch (start us, length us, event | category | flops | bytes accessed | tf_op | source)
XLA Modules:
  0.0 202.7 jit_solution(2323071310931210941)
XLA Ops:
  7.2 0.0 copy-start
  7.2 4.2 %copy.20 = bf16[256,4096]{0,1:T(8,128)(2,1)} copy(bf16[256,4096]{1,0:T(8,128)(2,1)} %param.7) | data formatting | bytes 4194304 | tf_op args[0]
  11.4 1.9 constant_dynamic-slice_fusion
  13.3 6.3 %all-to-all-start = ((bf16[256,8,128]{0,2,1:T(8,128)(2,1)}), bf16[256,8,128]{0,2,1:T(8,128)(2,1)S(1)}, u32[]{:S(2)}, u32[]{:S(2)}) async-start(bf16[256,8,128]{0,2,1:T(8,128)(2,1)} %constant_dynamic-slice_fusion), calls=%async_computation.1 | async-start | bytes 1048576 | tf_op jit(solution)/shard_map/all_to_all | solution.py:476
  19.6 0.0 all-gather.2.cloned.1.call-start
  19.7 6.3 %convolution_bitcast_fusion = f32[32,8,8,128]{3,1,2,0:T(8,128)S(1)} fusion(bf16[256,4096]{1,0:T(8,128)(2,1)} %param.7, bf16[4096,1024]{1,0:T(8,128)(2,1)} %param.8), kind=kOutput, calls=%fused_computation.3 | convolution fusion | flops 2147483648 | bytes 11534336 | tf_op jit(solution)/shard_map/dot_general | solution.py:486
  26.0 0.0 copy-start.6
  26.0 0.2 copy.25
  26.2 0.5 copy-done.6
  26.7 1.2 fusion.5
  27.9 0.5 subtract_convert_fusion
  28.4 0.0 copy-start.1
  28.4 0.3 pad_maximum_fusion
  28.7 0.9 copy.33
  29.6 0.0 copy-done
  29.6 0.6 copy-done.1
  30.2 1.0 fusion.8
  31.2 0.1 copy.24
  31.4 0.1 copy.23
  31.5 0.3 subtract_convert_fusion.2
  31.8 0.4 pad_maximum_fusion.3
  32.2 2.8 %all-to-all-done = bf16[256,8,128]{0,2,1:T(8,128)(2,1)S(1)} async-done(((bf16[256,8,128]{0,2,1:T(8,128)(2,1)}), bf16[256,8,128]{0,2,1:T(8,128)(2,1)S(1)}, u32[]{:S(2)}, u32[]{:S(2)}) %all-to-all-start) | async-done | bytes 524320 | tf_op jit(solution)/shard_map/all_to_all | solution.py:476
  35.0 1.0 copy.21
  36.0 0.0 all-gather.2.cloned.1.call-update
  36.0 0.0 reduce-scatter.2.cloned.1.call-start
  36.0 2.9 %convolution_convert_fusion = bf16[256,256]{1,0:T(8,128)(2,1)S(1)} fusion(bf16[256,4096]{1,0:T(8,128)(2,1)} %param.7, bf16[4096,256]{1,0:T(8,128)(2,1)} %param.10), kind=kOutput, calls=%fused_computation.4 | convolution fusion | flops 536936448 | bytes 4325376 | tf_op jit(solution)/shard_map/dot_general | solution.py:486
  39.0 0.7 pad_maximum_fusion.1.own
  39.7 23.5 %shard_map.102 = bf16[8,256,512]{2,1,0:T(8,128)(2,1)} custom-call(bf16[256,512]{1,0:T(8,128)(2,1)} %pad_maximum_fusion.1.own), custom_call_target="tpu_custom_call" | custom-call | bytes 25165824 | tf_op jit(solution)/shard_map/pallas_call | solution.py:120
  63.2 1.0 multiply_sine_fusion.1
  64.1 52.4 %shard_map.103 = (bf16[256,1024]{1,0:T(8,128)(2,1)}, bf16[8,256,1024]{2,1,0:T(8,128)(2,1)}, bf16[2048,512]{1,0:T(8,128)(2,1)}) custom-call(s32[2,16]{1,0:T(2,128)} %mask.1, s32[1]{0:T(128)} %bitcast.first, bf16[256,1024]{1,0:T(8,128)(2,1)} %bitcast.53, bf16[256,1024]{1,0:T(8,128)(2,1)} %g.1, bf16[2048,512]{1,0:T(8,128)(2,1)} %bitcast.43, ...), custom_call_target="tpu_custom_call" | custom-call | flops 5368709120 | bytes 4194304 | tf_op jit(solution)/shard_map/pallas_call | solution.py:410
  116.6 0.0 copy-start.5
  116.6 0.0 copy-start.9
  116.6 26.0 %shard_map.104 = f32[256,512]{1,0:T(8,128)} custom-call(bf16[8,256,512]{2,1,0:T(8,128)(2,1)} %bitcast.41), custom_call_target="tpu_custom_call" | custom-call | bytes 25165824 | tf_op jit(solution)/shard_map/pallas_call | solution.py:201
  142.5 1.0 slice.35
  143.5 0.1 reshape.123
  143.7 0.0 copy-done.5
  143.7 0.5 subtract_convert_fusion.1
  144.2 0.4 pad_maximum_fusion.4
  144.5 0.0 copy-done.9
  144.5 5.7 %fusion.9 = f32[256,4096]{1,0:T(8,128)S(1)} fusion(bf16[256,1024]{1,0:T(8,128)(2,1)S(1)} %copy-done.9, bf16[4096,1024]{1,0:T(8,128)(2,1)} %param.8), kind=kOutput, calls=%fused_computation.34 | convolution fusion | flops 2147483648 | bytes 13107200 | tf_op jit(solution)/shard_map/dot_general | solution.py:215
  150.3 0.0 copy-start.2
  150.3 0.0 copy-start.4
  150.3 0.7 convolution_add_fusion.1
  151.1 0.3 copy-done.2
  151.3 0.7 copy-done.4
  152.1 2.1 %fusion = bf16[256,4096]{1,0:T(8,128)(2,1)} fusion(f32[256,4096]{1,0:T(8,128)S(1)} %convolution_add_fusion.1, bf16[4096,256]{1,0:T(8,128)(2,1)S(1)} %copy-done.4, f32[256,512]{1,0:T(8,128)S(1)} %copy-done.2), kind=kOutput, calls=%fused_computation.2 | convolution fusion | flops 538968064 | bytes 8519680 | tf_op jit(solution)/shard_map/dot_general | solution.py:215
  154.2 0.0 reduce-scatter.2.cloned.1.call-update
  154.3 0.7 pad_maximum_fusion.2.own
  155.0 31.2 %shard_map.105 = bf16[8,256,512]{2,1,0:T(8,128)(2,1)} custom-call(bf16[256,512]{1,0:T(8,128)(2,1)} %pad_maximum_fusion.2.own), custom_call_target="tpu_custom_call" | custom-call | bytes 25165824 | tf_op jit(solution)/shard_map/pallas_call | solution.py:120
  186.2 0.0 all-gather.2.cloned.1.call-done
  186.2 0.0 copy-start.3
  186.3 0.0 copy-start.7
  186.3 3.6 %fusion.3 = f32[512,256]{1,0:T(8,128)} fusion(bf16[2048,512]{1,0:T(8,128)(2,1)} %all-gather.2.cloned.1.call-done, bf16[2048,512]{1,0:T(8,128)(2,1)} %bitcast.45), kind=kOutput, calls=%fused_computation.7 | convolution fusion | flops 536870912 | bytes 3670016 | tf_op jit(solution)/shard_map/dot_general | solution.py:215
  189.8 0.0 copy-done.3
  189.8 0.0 copy-done.7
  189.8 0.0 copy-start.8
  189.8 1.5 fusion.1
  191.4 0.9 copy-done.8
  192.2 3.7 %fusion.10 = f32[512,1024]{1,0:T(8,128)} fusion(bf16[2048,512]{1,0:T(8,128)(2,1)S(1)} %copy-done.7, bf16[2048,1024]{1,0:T(8,128)(2,1)S(1)} %bitcast.56), kind=kOutput, calls=%fused_computation.35 | convolution fusion | flops 2147483648 | bytes 8388608 | tf_op jit(solution)/shard_map/dot_general | solution.py:215
  195.9 0.0 reduce-scatter.2.cloned.1.call-done
  (6 shorter events, 0.1 us)
Async XLA Ops:
  7.2 22.5 %copy-start = (bf16[4096,256]{1,0:T(8,128)(2,1)S(1)}, bf16[4096,256]{1,0:T(8,128)(2,1)}, u32[]{:S(2)}) copy-start(bf16[4096,256]{1,0:T(8,128)(2,1)} %param.9) | copy-start | bytes 6291460
  13.3 21.7 %all-to-all-start = ((bf16[256,8,128]{0,2,1:T(8,128)(2,1)}), bf16[256,8,128]{0,2,1:T(8,128)(2,1)S(1)}, u32[]{:S(2)}, u32[]{:S(2)}) async-start(bf16[256,8,128]{0,2,1:T(8,128)(2,1)} %constant_dynamic-slice_fusion), calls=%async_computation.1 | async-start | bytes 1048576 | tf_op jit(solution)/shard_map/all_to_all | solution.py:476
  19.6 166.6 %all-gather.2.cloned.1.call-start = ((), (), s32[]{:S(2)}) async-start(), calls=%async_computation.3 | async-start | bytes 2621440 | tf_op jit(solution)/shard_map/all_gather | solution.py:479
  26.0 0.7 copy-start.6
  28.4 1.8 copy-start.1
  36.0 159.9 %reduce-scatter.2.cloned.1.call-start = ((), (), s32[]{:S(2)}) async-start(), calls=%async_computation.2 | async-start | bytes 2621440 | tf_op jit(solution)/shard_map/reduce_scatter | solution.py:502
  116.6 27.1 %copy-start.5 = (f32[256,64]{1,0:T(8,128)S(1)}, f32[256,64]{1,0:T(8,128)}, u32[]{:S(2)}) copy-start(f32[256,64]{1,0:T(8,128)} %get-tuple-element.18) | copy-start | bytes 196612
  116.6 28.0 %copy-start.9 = (bf16[256,1024]{1,0:T(8,128)(2,1)S(1)}, bf16[256,1024]{1,0:T(8,128)(2,1)}, u32[]{:S(2)}) copy-start(bf16[256,1024]{1,0:T(8,128)(2,1)} %get-tuple-element.7) | copy-start | bytes 1572868
  150.3 1.0 copy-start.2
  150.3 1.8 copy-start.4
  186.2 3.6 %copy-start.3 = (bf16[8,256,512]{2,1,0:T(8,128)(2,1)S(1)}, bf16[8,256,512]{2,1,0:T(8,128)(2,1)}, u32[]{:S(2)}) copy-start(bf16[8,256,512]{2,1,0:T(8,128)(2,1)} %shard_map.105) | copy-start | bytes 6291460
  186.3 3.6 %copy-start.7 = (bf16[2048,512]{1,0:T(8,128)(2,1)S(1)}, bf16[2048,512]{1,0:T(8,128)(2,1)}, u32[]{:S(2)}) copy-start(bf16[2048,512]{1,0:T(8,128)(2,1)} %all-gather.2.cloned.1.call-done) | copy-start | bytes 6291460
  189.8 2.4 %copy-start.8 = (bf16[8,256,1024]{2,1,0:T(8,128)(2,1)S(1)}, bf16[8,256,1024]{2,1,0:T(8,128)(2,1)}, u32[]{:S(2)}) copy-start(bf16[8,256,1024]{2,1,0:T(8,128)(2,1)} %get-tuple-element.9) | copy-start | bytes 12582916
Sparse Core Ops, SparseCore 0:
  36.1 34.0 all-gather.1
  154.3 40.9 reduce-scatter.1

commit v4 on v3

--- a/solution.py
+++ b/solution.py
@@ -455,6 +455,24 @@
     )(mask, first, queries, grad_attn, keys_values, keys_values, cos_t, sin_t)
 
 
+def take_kernel(index, source, out):
+    out[...] = source[...]
+
+
+def take_columns(normed, index, devices, groups, part):
+    tokens = normed.shape[0]
+    return pl.pallas_call(
+        take_kernel,
+        out_shape=jax.ShapeDtypeStruct((devices * tokens, part), normed.dtype),
+        grid_spec=pltpu.PrefetchScalarGridSpec(
+            num_scalar_prefetch=1,
+            grid=(devices,),
+            in_specs=[pl.BlockSpec((tokens, part), lambda d, at: (0, d * groups + at[0]))],
+            out_specs=pl.BlockSpec((tokens, part), lambda d, at: (d, 0)),
+        ),
+    )(index.astype(jnp.int32).reshape(1), normed)
+
+
 def rotate(values, cosine, sine):
     rows = values.shape[0]
     pieces = values.reshape(rows, -1, HEAD)
@@ -470,12 +488,14 @@
     q_cols = w_query.shape[1]
     me = lax.axis_index("seq")
     part = width // devices // groups
-    my_part = lax.dynamic_slice_in_dim(
-        normed.reshape(tokens, devices, groups * part), lax.axis_index("kvh") * part, part, 2
-    )
-    columns = lax.all_to_all(
-        my_part.reshape(tokens, devices * part), "seq", split_axis=1, concat_axis=0, tiled=True
-    )
+    index = lax.axis_index("kvh")
+    if part % HEAD == 0:
+        pieces = take_columns(normed, index, devices, groups, part)
+    else:
+        wide = normed.reshape(tokens, devices, groups * part)
+        pieces = lax.dynamic_slice_in_dim(wide, index * part, part, 2)
+        pieces = jnp.transpose(pieces, (1, 0, 2)).reshape(devices * tokens, part)
+    columns = lax.all_to_all(pieces, "seq", split_axis=0, concat_axis=0, tiled=True)
     columns = lax.all_gather(columns, "kvh", axis=1, tiled=True)
 
     frequency = THETA ** (-(jnp.arange(HALF, dtype=jnp.float32) * (2.0 / HEAD)))

time: 203 us -> 202 us (level)
  local copies, waits for them, and re-layouts: 12.6 us -> 6.31 us
  Pallas kernels: 133 us -> 138 us
    pallas_call x0 -> x1, Pallas kernels: none -> 4.9 us  [take_columns(): pl.pallas_call(take_kernel, out_shape=jax.ShapeDtypeStruct((devices * tok...]
    unnamed x27 -> x28, local copies, waits for them, and re-layouts: 8.59 us -> 5.17 us
where the time goes in v4:
time: 202 us; the launch traced here: 201 us
  Pallas kernels  138 us (68%)
  matrix products  27.6 us (14%)
  between operations  14.3 us (7%)
  starting transfers between devices  6.4 us (3%)
  local copies, waits for them, and re-layouts  6.31 us (3%)
  other arithmetic  5.88 us (3%)
  waiting for transfers between devices  2.82 us (1%)
    pallas_call x2, Pallas kernels, gather(): pl.pallas_call(functools.partial(gather_kernel, chips), out_shape=jax.Sha...  54.7 us
    pallas_call x1, Pallas kernels, attention(): pl.pallas_call(functools.partial(attention_kernel, group, 512, chips, pai...  52.4 us
    pallas_call x1, Pallas kernels, reduce_to_owner(): pl.pallas_call(functools.partial(reduce_kernel, chips), out_shape=jax.Sha...  26 us
    dot_general x6, matrix products, dot(): lax.dot_general(left, right, ((contract[:1], contract[1:]), ((), ())), pr...  17.4 us
    dot_general x3, matrix products, project(): return jnp.dot(normed, weight, preferred_element_type=jnp.float32)  10.3 us
    all_to_all x1, starting transfers between devices, body(): lax.all_to_all(pieces, 'seq', split_axis=0, concat_axis=0, tiled=True)  6.33 us
    unnamed x28, local copies, waits for them, and re-layouts  5.17 us
    pallas_call x1, Pallas kernels, take_columns(): pl.pallas_call(take_kernel, out_shape=jax.ShapeDtypeStruct((devices * tok...  4.9 us
  transfers between devices with their start and end apart: 3, of which 1 were waited for; matrix products, arithmetic and copies ran while one was open for 18% of the time, Pallas kernels for 66%

profile of v4, /device:TPU:0, one launch (start us, length us, event | category | flops | bytes accessed | tf_op | source)
XLA Modules:
  0.0 201.4 jit_solution(17092579586419083671)
XLA Ops:
  7.2 0.0 copy-start
  7.2 4.9 %shard_map.105 = bf16[2048,128]{1,0:T(8,128)(2,1)} custom-call(s32[1]{0:T(128)} %bitcast.4.index, bf16[256,4096]{1,0:T(8,128)(2,1)} %source.1), custom_call_target="tpu_custom_call" | custom-call | tf_op jit(solution)/shard_map/pallas_call | solution.py:464
  12.1 6.3 %all-to-all-start = ((bf16[8,256,128]{2,1,0:T(8,128)(2,1)}), bf16[8,256,128]{2,1,0:T(8,128)(2,1)S(1)}, u32[]{:S(2)}, u32[]{:S(2)}) async-start(bf16[8,256,128]{2,1,0:T(8,128)(2,1)} %bitcast.47), calls=%async_computation.1 | async-start | bytes 1048576 | tf_op jit(solution)/shard_map/all_to_all | solution.py:498
  18.4 0.0 all-gather.2.cloned.1.call-start
  18.5 6.3 %convolution_bitcast_fusion = f32[32,8,8,128]{3,1,2,0:T(8,128)S(1)} fusion(bf16[256,4096]{1,0:T(8,128)(2,1)} %source.1, bf16[4096,1024]{1,0:T(8,128)(2,1)} %param.8), kind=kOutput, calls=%fused_computation.3 | convolution fusion | flops 2147483648 | bytes 11534336 | tf_op jit(solution)/shard_map/dot_general | solution.py:506
  24.8 0.0 copy-start.7
  24.8 0.2 copy.17
  25.0 0.5 copy-done.7
  25.5 1.2 fusion.5
  26.7 0.5 subtract_convert_fusion
  27.2 0.0 copy-start.1
  27.2 0.3 pad_maximum_fusion
  27.5 0.9 copy.25
  28.4 0.0 copy-done
  28.4 0.6 copy-done.1
  29.0 1.0 fusion.8
  30.0 0.1 copy.16
  30.2 0.1 copy.15
  30.3 0.3 subtract_convert_fusion.2
  30.6 0.4 pad_maximum_fusion.3
  31.0 2.8 %all-to-all-done = bf16[8,256,128]{2,1,0:T(8,128)(2,1)S(1)} async-done(((bf16[8,256,128]{2,1,0:T(8,128)(2,1)}), bf16[8,256,128]{2,1,0:T(8,128)(2,1)S(1)}, u32[]{:S(2)}, u32[]{:S(2)}) %all-to-all-start) | async-done | bytes 524320 | tf_op jit(solution)/shard_map/all_to_all | solution.py:498
  33.8 0.0 copy-start.4
  33.8 0.8 copy-done.4
  34.6 0.0 all-gather.2.cloned.1.call-update
  34.6 0.0 reduce-scatter.2.cloned.1.call-start
  34.6 2.9 %convolution_convert_fusion = bf16[256,256]{1,0:T(8,128)(2,1)S(1)} fusion(bf16[256,4096]{1,0:T(8,128)(2,1)} %source.1, bf16[4096,256]{1,0:T(8,128)(2,1)} %param.10), kind=kOutput, calls=%fused_computation.4 | convolution fusion | flops 536936448 | bytes 4325376 | tf_op jit(solution)/shard_map/dot_general | solution.py:506
  37.6 0.7 pad_maximum_fusion.1.own
  38.3 23.5 %shard_map.102 = bf16[8,256,512]{2,1,0:T(8,128)(2,1)} custom-call(bf16[256,512]{1,0:T(8,128)(2,1)} %pad_maximum_fusion.1.own), custom_call_target="tpu_custom_call" | custom-call | bytes 25165824 | tf_op jit(solution)/shard_map/pallas_call | solution.py:120
  61.8 1.0 multiply_sine_fusion.1
  62.7 52.4 %shard_map.103 = (bf16[256,1024]{1,0:T(8,128)(2,1)}, bf16[8,256,1024]{2,1,0:T(8,128)(2,1)}, bf16[2048,512]{1,0:T(8,128)(2,1)}) custom-call(s32[2,16]{1,0:T(2,128)} %mask.1, s32[1]{0:T(128)} %bitcast.first, bf16[256,1024]{1,0:T(8,128)(2,1)} %bitcast.52, bf16[256,1024]{1,0:T(8,128)(2,1)} %g.1, bf16[2048,512]{1,0:T(8,128)(2,1)} %bitcast.42, ...), custom_call_target="tpu_custom_call" | custom-call | flops 5368709120 | bytes 4194304 | tf_op jit(solution)/shard_map/pallas_call | solution.py:410
  115.2 0.0 copy-start.6
  115.2 0.0 copy-start.10
  115.2 26.0 %shard_map.104 = f32[256,512]{1,0:T(8,128)} custom-call(bf16[8,256,512]{2,1,0:T(8,128)(2,1)} %bitcast.40), custom_call_target="tpu_custom_call" | custom-call | bytes 25165824 | tf_op jit(solution)/shard_map/pallas_call | solution.py:201
  141.1 1.0 slice.35
  142.1 0.1 reshape.120
  142.3 0.0 copy-done.6
  142.3 0.5 subtract_convert_fusion.1
  142.8 0.4 pad_maximum_fusion.4
  143.1 0.0 copy-done.10
  143.1 5.8 %fusion.9 = f32[256,4096]{1,0:T(8,128)S(1)} fusion(bf16[256,1024]{1,0:T(8,128)(2,1)S(1)} %copy-done.10, bf16[4096,1024]{1,0:T(8,128)(2,1)} %param.8), kind=kOutput, calls=%fused_computation.33 | convolution fusion | flops 2147483648 | bytes 13107200 | tf_op jit(solution)/shard_map/dot_general | solution.py:215
  148.9 0.0 copy-start.2
  148.9 0.0 copy-start.5
  148.9 0.7 convolution_add_fusion.1
  149.7 0.3 copy-done.2
  149.9 0.7 copy-done.5
  150.7 2.1 %fusion = bf16[256,4096]{1,0:T(8,128)(2,1)} fusion(f32[256,4096]{1,0:T(8,128)S(1)} %convolution_add_fusion.1, bf16[4096,256]{1,0:T(8,128)(2,1)S(1)} %copy-done.5, f32[256,512]{1,0:T(8,128)S(1)} %copy-done.2), kind=kOutput, calls=%fused_computation.2 | convolution fusion | flops 538968064 | bytes 8519680 | tf_op jit(solution)/shard_map/dot_general | solution.py:215
  152.8 0.0 reduce-scatter.2.cloned.1.call-update
  152.9 0.7 pad_maximum_fusion.2.own
  153.6 31.2 %shard_map.106 = bf16[8,256,512]{2,1,0:T(8,128)(2,1)} custom-call(bf16[256,512]{1,0:T(8,128)(2,1)} %pad_maximum_fusion.2.own), custom_call_target="tpu_custom_call" | custom-call | bytes 25165824 | tf_op jit(solution)/shard_map/pallas_call | solution.py:120
  184.8 0.0 all-gather.2.cloned.1.call-done
  184.8 0.0 copy-start.3
  184.9 0.0 copy-start.8
  184.9 3.6 %fusion.3 = f32[512,256]{1,0:T(8,128)} fusion(bf16[2048,512]{1,0:T(8,128)(2,1)} %all-gather.2.cloned.1.call-done, bf16[2048,512]{1,0:T(8,128)(2,1)} %bitcast.44), kind=kOutput, calls=%fused_computation.7 | convolution fusion | flops 536870912 | bytes 3670016 | tf_op jit(solution)/shard_map/dot_general | solution.py:215
  188.4 0.0 copy-done.3
  188.4 0.0 copy-done.8
  188.4 0.0 copy-start.9
  188.4 1.5 fusion.1
  190.0 0.9 copy-done.9
  190.8 3.7 %fusion.10 = f32[512,1024]{1,0:T(8,128)} fusion(bf16[2048,512]{1,0:T(8,128)(2,1)S(1)} %copy-done.8, bf16[2048,1024]{1,0:T(8,128)(2,1)S(1)} %bitcast.55), kind=kOutput, calls=%fused_computation.34 | convolution fusion | flops 2147483648 | bytes 8388608 | tf_op jit(solution)/shard_map/dot_general | solution.py:215
  194.5 0.0 reduce-scatter.2.cloned.1.call-done
  (6 shorter events, 0.1 us)
Async XLA Ops:
  7.2 21.3 %copy-start = (bf16[4096,256]{1,0:T(8,128)(2,1)S(1)}, bf16[4096,256]{1,0:T(8,128)(2,1)}, u32[]{:S(2)}) copy-start(bf16[4096,256]{1,0:T(8,128)(2,1)} %param.9) | copy-start | bytes 6291460
  12.1 21.7 %all-to-all-start = ((bf16[8,256,128]{2,1,0:T(8,128)(2,1)}), bf16[8,256,128]{2,1,0:T(8,128)(2,1)S(1)}, u32[]{:S(2)}, u32[]{:S(2)}) async-start(bf16[8,256,128]{2,1,0:T(8,128)(2,1)} %bitcast.47), calls=%async_computation.1 | async-start | bytes 1048576 | tf_op jit(solution)/shard_map/all_to_all | solution.py:498
  18.4 166.4 %all-gather.2.cloned.1.call-start = ((), (), s32[]{:S(2)}) async-start(), calls=%async_computation.3 | async-start | bytes 2621440 | tf_op jit(solution)/shard_map/all_gather | solution.py:499
  24.8 0.7 copy-start.7
  27.2 1.8 copy-start.1
  33.8 0.8 copy-start.4
  34.6 159.9 %reduce-scatter.2.cloned.1.call-start = ((), (), s32[]{:S(2)}) async-start(), calls=%async_computation.2 | async-start | bytes 2621440 | tf_op jit(solution)/shard_map/reduce_scatter | solution.py:522
  115.2 27.1 %copy-start.6 = (f32[256,64]{1,0:T(8,128)S(1)}, f32[256,64]{1,0:T(8,128)}, u32[]{:S(2)}) copy-start(f32[256,64]{1,0:T(8,128)} %get-tuple-element.18) | copy-start | bytes 196612
  115.2 28.0 %copy-start.10 = (bf16[256,1024]{1,0:T(8,128)(2,1)S(1)}, bf16[256,1024]{1,0:T(8,128)(2,1)}, u32[]{:S(2)}) copy-start(bf16[256,1024]{1,0:T(8,128)(2,1)} %get-tuple-element.7) | copy-start | bytes 1572868
  148.9 1.0 copy-start.2
  148.9 1.8 copy-start.5
  184.8 3.6 %copy-start.3 = (bf16[8,256,512]{2,1,0:T(8,128)(2,1)S(1)}, bf16[8,256,512]{2,1,0:T(8,128)(2,1)}, u32[]{:S(2)}) copy-start(bf16[8,256,512]{2,1,0:T(8,128)(2,1)} %shard_map.106) | copy-start | bytes 6291460
  184.9 3.6 %copy-start.8 = (bf16[2048,512]{1,0:T(8,128)(2,1)S(1)}, bf16[2048,512]{1,0:T(8,128)(2,1)}, u32[]{:S(2)}) copy-start(bf16[2048,512]{1,0:T(8,128)(2,1)} %all-gather.2.cloned.1.call-done) | copy-start | bytes 6291460
  188.4 2.4 %copy-start.9 = (bf16[8,256,1024]{2,1,0:T(8,128)(2,1)S(1)}, bf16[8,256,1024]{2,1,0:T(8,128)(2,1)}, u32[]{:S(2)}) copy-start(bf16[8,256,1024]{2,1,0:T(8,128)(2,1)} %get-tuple-element.9) | copy-start | bytes 12582916
Sparse Core Ops, SparseCore 0:
  34.7 34.0 all-gather.1
  152.9 40.9 reduce-scatter.1
